TPU v7x, 256 devices: a whole 4x4x8 slice. The times are simulated.
256 devices in a mesh: kern: 16 (over z_lo, x, core), slab: 16 (over y, z_hi).
Axes of the slice: x: 4, y: 4, z: 8 (z_hi: 4, z_lo: 2; z = z_hi * 2 + z_lo), core: 2. Of those that a mesh axis runs over, the one named last changes fastest.
Arguments:
- mask_params: float32 [2048, 2048], P('slab', 'kern'), may hold values from -6 to 6
- target_bits: int32 [2048, 2048], P('slab'), may hold values 0 or 1
- kernels: float32 [16, 2, 512, 512], P('kern', None, None, 'slab'), may hold values from -19.091883 to 19.091883
- weights: float32 [16], P('kern'), may hold values from 0.1 to 0.5
- dose_factors: float32 [2], replicated, may hold values from 0.25 to 1.75
Outputs:
- new_params: float32 [2048, 2048], P('slab', 'kern')
- resist_image: float32 [2, 2, 2048, 2048], P(None, None, 'slab', 'kern')
All inputs are finite; a program needn't handle non-finite values. No bound on the sum of `target_bits` on one device may be relied on, other than what follows from the above.
Results may differ from a plain program's by a relative error of at most 0.035.
Values may be sent and summed in bfloat16 or wider, within the bound.
A program may use at most 128 MiB of HBM per device.

v0:
```python
import math

import jax
import jax.numpy as jnp
from jax import lax
from jax.sharding import PartitionSpec as P

N = 2048
F = 512
FOCI = 2
STEPS = 2


steepness = 3.0
threshold = 1.0
step_rate = 0.4


def times_transposed(left, right):
    return lax.dot_general(
        left, right, (((1,), (1,)), ((), ())), preferred_element_type=jnp.float32
    )


def transposed_times(left, right):
    return lax.dot_general(
        left, right, (((0,), (0,)), ((), ())), preferred_element_type=jnp.float32
    )


def plain_product(left, right):
    return jnp.dot(left, right, preferred_element_type=jnp.float32)


def tables():
    freqs = jnp.arange(F, dtype=jnp.int32) - F // 2
    pixels = jnp.arange(N, dtype=jnp.int32)
    phases = freqs[:, None] * pixels[None, :] % N
    angles = phases.astype(jnp.float32) * (2.0 * math.pi / N)
    scale = 1.0 / math.sqrt(N)
    return (
        (jnp.cos(angles) * scale).astype(jnp.bfloat16),
        (jnp.sin(angles) * scale).astype(jnp.bfloat16),
    )


def resist(intensity, dose_factors, target_float):
    dose_grid = dose_factors[None, :, None, None]
    printed = jax.nn.sigmoid(steepness * (dose_grid * intensity[:, None] - threshold))
    errors = (printed - target_float) * printed * (1.0 - printed) * steepness * dose_grid
    return (printed, jnp.sum(errors, axis=1))


def body(mask_params, target_bits, kernels, weights, dose_factors):
    row_count = mask_params.shape[0]
    col_block = mask_params.shape[1]
    local_kernels = kernels.shape[0]
    cosine_table, sine_table = tables()
    stacked_table = jnp.concatenate([cosine_table, sine_table], axis=0)
    start_row = lax.axis_index("slab") * row_count
    start_col = lax.axis_index("kern") * col_block
    first_kernel = lax.axis_index("kern") * local_kernels
    cosine_rows = lax.dynamic_slice_in_dim(cosine_table, start_row, row_count, 1)
    sine_rows = lax.dynamic_slice_in_dim(sine_table, start_row, row_count, 1)
    stacked_rows = jnp.concatenate([cosine_rows, sine_rows], axis=0)
    target_float = target_bits.astype(jnp.float32)
    foci_ids = jnp.arange(FOCI, dtype=jnp.int32)
    selectors = [(foci_ids == (first_kernel + 0) % FOCI).astype(jnp.float32)]
    params = mask_params
    printed_block = None
    for iteration in range(STEPS):
        mask_values = jnp.tanh(params)
        mask_full = lax.all_gather(mask_values.astype(jnp.bfloat16), "kern", axis=1, tiled=True)
        column_spec = times_transposed(mask_full, stacked_table)
        spec_input = jnp.stack([column_spec[:, :F], -column_spec[:, F:]]).astype(jnp.bfloat16)
        part_real = plain_product(stacked_rows, spec_input[0])
        part_imag = plain_product(stacked_rows, spec_input[1])
        spectrum = lax.psum_scatter(
            jnp.stack([part_real[:F] + part_imag[F:], part_imag[:F] - part_real[F:]]).astype(
                jnp.bfloat16
            ),
            "slab",
            scatter_dimension=2,
            tiled=True,
        ).astype(jnp.float32)
        spec_real = spectrum[0]
        spec_imag = spectrum[1]
        kernel_slot = 0
        kernel_real = kernels[kernel_slot, 0]
        kernel_imag = kernels[kernel_slot, 1]
        filtered = jnp.stack(
            [
                kernel_real * spec_real - kernel_imag * spec_imag,
                kernel_real * spec_imag + kernel_imag * spec_real,
            ]
        ).astype(jnp.bfloat16)
        filtered_full = lax.all_gather(filtered, "slab", axis=2, tiled=True)
        joined = jnp.concatenate([filtered_full[0], filtered_full[1]], axis=1)
        cos_part = transposed_times(cosine_rows, joined)
        sin_part = transposed_times(sine_rows, joined)
        inverse_rows = jnp.stack(
            [cos_part[:, :F] - sin_part[:, F:], cos_part[:, F:] + sin_part[:, :F]]
        ).astype(jnp.bfloat16)
        flat_rows = inverse_rows.reshape(2 * row_count, F)
        with_cosine = plain_product(flat_rows, cosine_table)
        with_sine = plain_product(flat_rows, sine_table)
        field_real = with_cosine[:row_count] - with_sine[row_count:]
        field_imag = with_sine[:row_count] + with_cosine[row_count:]
        saved_fields = [(field_real, field_imag)]
        power = weights[kernel_slot] * (field_real * field_real + field_imag * field_imag)
        intensity_terms = selectors[kernel_slot][:, None, None] * power[None]
        intensity_full = lax.psum(intensity_terms.astype(jnp.bfloat16), "kern").astype(jnp.float32)
        printed_full, sens_full = resist(intensity_full, dose_factors, target_float)
        printed_block = lax.dynamic_slice_in_dim(printed_full, start_col, col_block, 3)
        kernel_slot = 0
        kernel_real = kernels[kernel_slot, 0]
        kernel_imag = kernels[kernel_slot, 1]
        field_real, field_imag = saved_fields[kernel_slot]
        kernel_sens = jnp.sum(selectors[kernel_slot][:, None, None] * sens_full, axis=0)
        scaled_sens = 2.0 * weights[kernel_slot] * kernel_sens
        cotangent = jnp.stack([scaled_sens * field_real, scaled_sens * field_imag]).astype(
            jnp.bfloat16
        )
        flat_cot = cotangent.reshape(2 * row_count, N)
        with_cosine = times_transposed(flat_cot, cosine_table)
        with_sine = times_transposed(flat_cot, sine_table)
        back_rows = jnp.stack(
            [
                with_cosine[:row_count] + with_sine[row_count:],
                with_cosine[row_count:] - with_sine[:row_count],
            ]
        ).astype(jnp.bfloat16)
        part_real = plain_product(stacked_rows, back_rows[0])
        part_imag = plain_product(stacked_rows, back_rows[1])
        grad_spec = lax.psum_scatter(
            jnp.stack([part_real[:F] + part_imag[F:], part_imag[:F] - part_real[F:]]).astype(
                jnp.bfloat16
            ),
            "slab",
            scatter_dimension=2,
            tiled=True,
        ).astype(jnp.float32)
        grad_real = grad_spec[0]
        grad_imag = grad_spec[1]
        spec_cotangent = jnp.stack(
            [
                kernel_real * grad_real + kernel_imag * grad_imag,
                kernel_real * grad_imag - kernel_imag * grad_real,
            ]
        ).astype(jnp.bfloat16)
        cot_full = lax.all_gather(spec_cotangent, "slab", axis=2, tiled=True)
        joined = jnp.concatenate([cot_full[0], cot_full[1]], axis=1)
        cos_part = transposed_times(cosine_rows, joined)
        sin_part = transposed_times(sine_rows, joined)
        adj_rows = jnp.stack(
            [cos_part[:, :F] - sin_part[:, F:], sin_part[:, :F] + cos_part[:, F:]]
        ).astype(jnp.bfloat16)
        mask_grad = plain_product(adj_rows[0], cosine_table) - plain_product(
            adj_rows[1], sine_table
        )
        grad_block = lax.psum_scatter(
            mask_grad.astype(jnp.bfloat16), "kern", scatter_dimension=1, tiled=True
        ).astype(jnp.float32)
        params = params - step_rate * grad_block * (1.0 - mask_values * mask_values)
    return (params, printed_block)


def solution(mesh):
    in_specs = (P("slab", "kern"), P("slab", None), P("kern", None, None, "slab"), P("kern"), P())
    out_specs = (P("slab", "kern"), P(None, None, "slab", "kern"))
    return jax.shard_map(body, mesh=mesh, in_specs=in_specs, out_specs=out_specs, check_vma=False)
```

profile of v0, /device:TPU:1, one launch (start us, length us, event | category | flops | bytes accessed | tf_op | source)
XLA Modules:
  0.0 1609.0 jit_solution(3888602054886694564)
XLA Ops:
  8.1 22.8 %all_gather.18 = bf16[128,2048]{1,0:T(8,128)(2,1)S(1)} all-gather(bf16[128,128]{1,0:T(8,128)(2,1)S(1)} %tanh_convert_fusion.1), channel_id=1, replica_groups=mesh['kern'=16,'slab'=16] {'kern'}, dimensions={1}, use_global_device_ids=true | all-gather | bytes 557056 | tf_op jit(solution)/shard_map/all_gather | solution.py:73
  30.9 18.8 %multiply_convert_fusion.1 = (bf16[512,2048]{1,0:T(8,128)(2,1)S(1)}, bf16[512,2048]{1,0:T(8,128)(2,1)}) fusion(s32[512]{0:T(512)S(1)} %iota_add_fusion), kind=kLoop, calls=%fused_computation.17 | loop fusion | flops 18874368 | bytes 4196352 | tf_op jit(solution)/shard_map/convert_element_type | solution.py:42
  59.4 158.4 %all-reduce.15.cloned.1.call-done = bf16[2,512,512]{1,0,2:T(2,128)(2,1)} async-done(((bf16[2,512,512]{1,0,2:T(2,128)(2,1)}), bf16[2,512,512]{1,0,2:T(2,128)(2,1)}) %all-reduce.15.cloned.1.call-update) | async-done | bytes 1048592
  220.4 60.2 %all-gather.5.cloned.1.call-done = bf16[2,512,512]{1,0,2:T(2,128)(2,1)} async-done(((bf16[2,512,32]{1,0,2:T(2,128)(2,1)}), bf16[2,512,512]{1,0,2:T(2,128)(2,1)}) %all-gather.5.cloned.1.call-update) | async-done | bytes 1048592 | tf_op jit(solution)/shard_map/all_gather | solution.py:97
  287.9 16.0 fusion.25
  324.3 121.1 %all-reduce.11.cloned.1.call-done = bf16[2,128,2048]{2,1,0:T(8,128)(2,1)} async-done(((bf16[2,128,2048]{2,1,0:T(8,128)(2,1)}), bf16[2,128,2048]{2,1,0:T(8,128)(2,1)}) %all-reduce.11.cloned.1.call-update) | async-done | bytes 1048592 | tf_op jit(solution)/shard_map/psum | solution.py:112
  450.4 16.3 %fusion.24 = f32[256,512]{1,0:T(8,128)S(1)} fusion(bf16[256,2048]{1,0:T(8,128)(2,1)S(1)} %bitcast.111, s32[512]{0:T(512)S(1)} %iota_add_fusion), kind=kOutput, calls=%fused_computation.39 | convolution fusion | flops 553648128 | bytes 1574912 | tf_op jit(solution)/shard_map/dot_general | solution.py:20
  466.7 16.3 %fusion.20 = f32[256,512]{1,0:T(8,128)S(1)} fusion(bf16[256,2048]{1,0:T(8,128)(2,1)S(1)} %bitcast.112, s32[512]{0:T(512)S(1)} %iota_add_fusion), kind=kOutput, calls=%fused_computation.35 | convolution fusion | flops 553648128 | bytes 1574912 | tf_op jit(solution)/shard_map/dot_general | solution.py:20
  486.8 161.8 %all-reduce.17.cloned.1.call-done = bf16[2,512,512]{1,0,2:T(2,128)(2,1)} async-done(((bf16[2,512,512]{1,0,2:T(2,128)(2,1)}), bf16[2,512,512]{1,0,2:T(2,128)(2,1)}) %all-reduce.17.cloned.1.call-update) | async-done | bytes 1048592
  650.5 60.7 %all-gather.7.cloned.1.call-done = bf16[2,512,512]{1,0,2:T(2,128)(2,1)} async-done(((bf16[2,512,32]{1,0,2:T(2,128)(2,1)}), bf16[2,512,512]{1,0,2:T(2,128)(2,1)}) %all-gather.7.cloned.1.call-update) | async-done | bytes 1048592 | tf_op jit(solution)/shard_map/all_gather | solution.py:151
  721.2 16.1 fusion.19
  737.3 16.8 %fusion.14 = bf16[128,2048]{1,0:T(8,128)(2,1)} fusion(f32[128,2048]{1,0:T(8,128)S(1)} %fusion.19, s32[512]{0:T(512)S(1)} %iota_add_fusion, f32[128,1024]{1,0:T(8,128)S(1)} %fusion.40, f32[128,1024]{1,0:T(8,128)S(1)} %fusion.39), kind=kOutput, calls=%fused_computation.25 | convolution fusion | flops 285868032 | bytes 2099200 | tf_op jit(solution)/shard_map/dot_general | solution.py:32
  756.2 58.4 %reduce-scatter.7.cloned.1.call-done = bf16[128,128]{1,0:T(8,128)(2,1)} async-done(((bf16[2048,128]{1,0:T(8,128)(2,1)}), bf16[128,128]{1,0:T(8,128)(2,1)}) %reduce-scatter.7.cloned.1.call-update) | async-done | bytes 32784
  816.9 21.5 %all_gather.21 = bf16[128,2048]{1,0:T(8,128)(2,1)S(1)} all-gather(bf16[128,128]{1,0:T(8,128)(2,1)S(1)} %tanh_convert_fusion), channel_id=1, replica_groups=mesh['kern'=16,'slab'=16] {'kern'}, dimensions={1}, use_global_device_ids=true | all-gather | bytes 557056 | tf_op jit(solution)/shard_map/all_gather | solution.py:73
  845.3 158.9 %all-reduce.19.cloned.1.call-done = bf16[2,512,512]{1,0,2:T(2,128)(2,1)} async-done(((bf16[2,512,512]{1,0,2:T(2,128)(2,1)}), bf16[2,512,512]{1,0,2:T(2,128)(2,1)}) %all-reduce.19.cloned.1.call-update) | async-done | bytes 1048592
  1006.2 60.9 %all-gather.9.cloned.1.call-done = bf16[2,512,512]{1,0,2:T(2,128)(2,1)} async-done(((bf16[2,512,32]{1,0,2:T(2,128)(2,1)}), bf16[2,512,512]{1,0,2:T(2,128)(2,1)}) %all-gather.9.cloned.1.call-update) | async-done | bytes 1048592 | tf_op jit(solution)/shard_map/all_gather | solution.py:97
  1077.4 16.0 fusion.23
  1112.3 122.4 %all-reduce.13.cloned.1.call-done = bf16[2,128,2048]{2,1,0:T(8,128)(2,1)} async-done(((bf16[2,128,2048]{2,1,0:T(8,128)(2,1)}), bf16[2,128,2048]{2,1,0:T(8,128)(2,1)}) %all-reduce.13.cloned.1.call-update) | async-done | bytes 1048592 | tf_op jit(solution)/shard_map/psum | solution.py:112
  1241.2 16.3 %fusion.22 = f32[256,512]{1,0:T(8,128)S(1)} fusion(bf16[256,2048]{1,0:T(8,128)(2,1)S(1)} %bitcast.113, s32[512]{0:T(512)S(1)} %iota_add_fusion), kind=kOutput, calls=%fused_computation.37 | convolution fusion | flops 553648128 | bytes 1574912 | tf_op jit(solution)/shard_map/dot_general | solution.py:20
  1257.5 16.3 %fusion.17 = f32[256,512]{1,0:T(8,128)S(1)} fusion(bf16[256,2048]{1,0:T(8,128)(2,1)S(1)} %bitcast.114, s32[512]{0:T(512)S(1)} %iota_add_fusion), kind=kOutput, calls=%fused_computation.32 | convolution fusion | flops 553648128 | bytes 1574912 | tf_op jit(solution)/shard_map/dot_general | solution.py:20
  1277.5 161.6 %all-reduce.21.cloned.1.call-done = bf16[2,512,512]{1,0,2:T(2,128)(2,1)} async-done(((bf16[2,512,512]{1,0,2:T(2,128)(2,1)}), bf16[2,512,512]{1,0,2:T(2,128)(2,1)}) %all-reduce.21.cloned.1.call-update) | async-done | bytes 1048592
  1441.1 60.9 %all-gather.11.cloned.1.call-done = bf16[2,512,512]{1,0,2:T(2,128)(2,1)} async-done(((bf16[2,512,32]{1,0,2:T(2,128)(2,1)}), bf16[2,512,512]{1,0,2:T(2,128)(2,1)}) %all-gather.11.cloned.1.call-update) | async-done | bytes 1048592 | tf_op jit(solution)/shard_map/all_gather | solution.py:151
  1508.9 16.0 fusion.16
  1543.6 56.8 %reduce-scatter.9.cloned.1.call-done = bf16[128,128]{1,0:T(8,128)(2,1)} async-done(((bf16[2048,128]{1,0:T(8,128)(2,1)}), bf16[128,128]{1,0:T(8,128)(2,1)}) %reduce-scatter.9.cloned.1.call-update) | async-done | bytes 32784
  (136 shorter events, 141.1 us)
Async XLA Ops:
  7.2 210.6 %all-reduce.15.cloned.1.call-start = ((), (), s32[]{:S(2)}) async-start(), calls=%async_computation.10 | async-start | bytes 2097152
  49.7 3.6 copy-start.4
  55.2 2.9 copy-start.10
  55.2 4.1 copy-start.8
  58.0 222.6 %all-gather.5.cloned.1.call-start = ((), (), s32[]{:S(2)}) async-start(), calls=%async_computation.2 | async-start | bytes 1114112 | tf_op jit(solution)/shard_map/all_gather | solution.py:97
  219.7 225.7 %all-reduce.11.cloned.1.call-start = ((), (), s32[]{:S(2)}) async-start(), calls=%async_computation.3 | async-start | bytes 2097152 | tf_op jit(solution)/shard_map/psum | solution.py:112
  319.9 1.4 copy-start.2
  321.2 3.0 copy-start.9
  322.9 325.6 %all-reduce.17.cloned.1.call-start = ((), (), s32[]{:S(2)}) async-start(), calls=%async_computation.11 | async-start | bytes 2097152
  446.9 2.9 copy-start.3
  486.7 224.5 %all-gather.7.cloned.1.call-start = ((), (), s32[]{:S(2)}) async-start(), calls=%async_computation.4 | async-start | bytes 1114112 | tf_op jit(solution)/shard_map/all_gather | solution.py:151
  650.4 164.2 %reduce-scatter.7.cloned.1.call-start = ((), (), s32[]{:S(2)}) async-start(), calls=%async_computation.8 | async-start | bytes 557056
  737.2 101.2 %copy-start.5 = (bf16[512,2048]{1,0:T(8,128)(2,1)S(1)}, bf16[512,2048]{1,0:T(8,128)(2,1)}, u32[]{:S(2)}) copy-start(bf16[512,2048]{1,0:T(8,128)(2,1)} %copy-done.4) | copy-start | bytes 6291460
  756.1 248.1 %all-reduce.19.cloned.1.call-start = ((), (), s32[]{:S(2)}) async-start(), calls=%async_computation.12 | async-start | bytes 2097152
  845.3 221.9 %all-gather.9.cloned.1.call-start = ((), (), s32[]{:S(2)}) async-start(), calls=%async_computation.5 | async-start | bytes 1114112 | tf_op jit(solution)/shard_map/all_gather | solution.py:97
  1006.2 228.6 %all-reduce.13.cloned.1.call-start = ((), (), s32[]{:S(2)}) async-start(), calls=%async_computation.6 | async-start | bytes 2097152 | tf_op jit(solution)/shard_map/psum | solution.py:112
  1109.4 1.4 copy-start
  1112.3 326.9 %all-reduce.21.cloned.1.call-start = ((), (), s32[]{:S(2)}) async-start(), calls=%async_computation.13 | async-start | bytes 2097152
  1236.2 4.3 copy-start.1
  1277.5 224.5 %all-gather.11.cloned.1.call-start = ((), (), s32[]{:S(2)}) async-start(), calls=%async_computation.7 | async-start | bytes 1114112 | tf_op jit(solution)/shard_map/all_gather | solution.py:151
  1441.0 159.4 %reduce-scatter.9.cloned.1.call-start = ((), (), s32[]{:S(2)}) async-start(), calls=%async_computation.9 | async-start | bytes 557056
  1524.9 76.4 %copy-start.6 = (f32[128,128]{1,0:T(8,128)S(1)}, f32[128,128]{1,0:T(8,128)}, u32[]{:S(2)}) copy-start(f32[128,128]{1,0:T(8,128)} %param.5) | copy-start | bytes 196612
  1524.9 76.4 %copy-start.7 = (bf16[128,128]{1,0:T(8,128)(2,1)S(1)}, bf16[128,128]{1,0:T(8,128)(2,1)}, u32[]{:S(2)}) copy-start(bf16[128,128]{1,0:T(8,128)(2,1)} %copy.72) | copy-start | bytes 98308
Sparse Core Ops, SparseCore 0:
  58.1 159.6 all-reduce.14
  221.1 59.4 all-gather.4
  323.0 122.3 all-reduce.10
  486.8 161.6 all-reduce.16
  651.7 59.4 all-gather.6
  756.3 58.2 reduce-scatter.6
  845.4 158.8 all-reduce.18
  1007.6 59.5 all-gather.8
  1112.4 122.3 all-reduce.12
  1277.6 161.4 all-reduce.20
  1442.5 59.4 all-gather.10
  1542.1 58.2 reduce-scatter.8
where the time goes:
time: 1620 us; the launch traced here: 1610 us
  waiting for transfers between devices  1240 us (77%)
  matrix products  211 us (13%)
  other arithmetic  47.4 us (3%)
  local copies, waits for them, and re-layouts  47.1 us (3%)
  blocking collectives  44.3 us (3%)
  between operations  16.3 us (1%)
    unnamed x18, waiting for transfers between devices  756 us
    psum x2, waiting for transfers between devices, body(): lax.psum(intensity_terms.astype(jnp.bfloat16), 'kern').astype(jnp.float32)  244 us
    dot_general x16, matrix products, plain_product(): return jnp.dot(left, right, preferred_element_type=jnp.float32)  132 us
    all_gather x2, waiting for transfers between devices, body(): cot_full = lax.all_gather(spec_cotangent, 'slab', axis=2, tiled=True)  122 us
    all_gather x2, waiting for transfers between devices, body(): filtered_full = lax.all_gather(filtered, 'slab', axis=2, tiled=True)  121 us
    dot_general x6, matrix products, times_transposed(): lax.dot_general(left, right, (((1,), (1,)), ((), ())), preferred_element_...  71.9 us
    all_gather x2, blocking collectives, body(): lax.all_gather(mask_values.astype(jnp.bfloat16), 'kern', axis=1, tiled=True)  44.3 us
  transfers between devices with their start and end apart: 12, of which 12 were waited for; matrix products, arithmetic and copies ran while one was open for 0% of the time, Pallas kernels for 0%

commit v1 on v0

v1 whole, which is shorter than its diff:
```python
import math

import jax
import jax.numpy as jnp
import ml_dtypes
import numpy as np
from jax import lax
from jax.experimental import pallas as pl
from jax.experimental.pallas import tpu as pltpu
from jax.sharding import PartitionSpec as P

N = 2048
F = 512
STEPS = 2
HALF = N // 2
EVEN = F // 2
SLABS = 16
KERNS = 16
MATES = 8

steepness = 3.0
threshold = 1.0
step_rate = 0.4
MESH = pl.DeviceIdType.MESH


def tables():
    index = np.concatenate([np.arange(0, F, 2), np.arange(1, F, 2)])
    pixels = np.arange(HALF)

    def pair(index, pixels):
        phases = ((index[:, None] - F // 2) * pixels[None, :]) % N
        angles = phases * (2.0 * math.pi / N)
        scale = 1.0 / math.sqrt(N)
        return np.cos(angles) * scale, np.sin(angles) * scale

    cos, sin = pair(index, pixels)
    to_pixels = np.concatenate([cos, sin], 1)
    from_pixels = np.concatenate([cos[:EVEN].T, sin[:EVEN].T, cos[EVEN:].T, sin[EVEN:].T], 1)
    k, s, i = np.meshgrid(np.arange(16), np.arange(8), np.arange(8), indexing="ij")
    owned = (s * 128 + k * 8 + i).reshape(-1)
    to_owned = np.concatenate([cos[:, owned], sin[:, owned]], 1)
    c, s = cos.reshape(2, EVEN, HALF)[:, :, owned], sin.reshape(2, EVEN, HALF)[:, :, owned]
    both = np.concatenate([c, s], 1).reshape(2, 2 * EVEN, 16, 64)
    from_owned = both.transpose(2, 0, 3, 1).reshape(N, 2 * EVEN)
    c, s = cos.reshape(2, 16, 16, HALF), sin.reshape(2, 16, 16, HALF)
    mixed = np.stack([c, -s]).transpose(2, 0, 1, 3, 4).reshape(2 * F, HALF)
    cast = lambda table: np.ascontiguousarray(table).astype(np.float32).astype(ml_dtypes.bfloat16)
    return [cast(t) for t in (mixed.T, from_owned, to_pixels, from_pixels, to_owned, mixed)]


def dot(left, right):
    return jnp.dot(left, right, preferred_element_type=jnp.float32)


def low(value):
    return value.astype(jnp.bfloat16)


def lane_of(shape):
    return lax.broadcasted_iota(jnp.int32, shape, len(shape) - 1)


def mask_to_columns(lo, hi, table):
    out = dot(low(jnp.concatenate([lo + hi, lo - hi], 0)), table[:, :])
    odd = (lane_of((8, 2 * F)) // 16) % 2
    return jnp.where(odd == 0, out[:8], out[8:])


def columns_transposed(got):
    lo, hi = got[:8].reshape(64, 128), got[8:].reshape(64, 128)
    return jnp.concatenate([lo + hi, lo - hi], 0).T


def spectrum(got, table):
    wide = jnp.concatenate([got[k] for k in range(KERNS)], 1)
    first = (lane_of(wide.shape) % 128) < 64
    zero = jnp.zeros_like(wide)
    left = jnp.concatenate([jnp.where(first, wide, zero), jnp.where(first, zero, wide)], 0)
    out = dot(left, table[:, :])
    real, imag = [], []
    for par in range(2):
        part = out[64 * par : 64 * par + 64]
        real.append(part[:32, :EVEN] + part[32:, EVEN:])
        imag.append(part[32:, :EVEN] - part[:32, EVEN:])
    return jnp.concatenate(real, 1), jnp.concatenate(imag, 1)


def filtered(h_re, h_im, s_re, s_im):
    return low(jnp.concatenate([h_re * s_re - h_im * s_im, h_re * s_im + h_im * s_re], 0))


def rows_of(g, table, chunk):
    halves = []
    for par in range(2):
        left = g[:, par * EVEN : par * EVEN + EVEN]
        with_cos = dot(left, table[par * EVEN : par * EVEN + EVEN, chunk * 256 : chunk * 256 + 256])
        with_sin = dot(left, table[par * EVEN : par * EVEN + EVEN, HALF + chunk * 256 : HALF + chunk * 256 + 256])
        halves.append(jnp.concatenate([with_cos[:32] - with_sin[32:], with_cos[32:] + with_sin[:32]], 0))
    return low(halves[0] + halves[1]), low(halves[0] - halves[1])


def turn(block):
    return low(block.astype(jnp.float32).T)


def field(x, table, chunk):
    fields = []
    for par in range(2):
        left = jnp.concatenate(
            [x[:, par * EVEN : par * EVEN + EVEN], x[:, F + par * EVEN : F + par * EVEN + EVEN]], 0
        )
        with_cos = dot(left, table[par * EVEN : par * EVEN + EVEN, chunk * 256 : chunk * 256 + 256])
        with_sin = dot(left, table[par * EVEN : par * EVEN + EVEN, HALF + chunk * 256 : HALF + chunk * 256 + 256])
        fields.append((with_cos[:128] - with_sin[128:], with_cos[128:] + with_sin[:128]))
    (e_re, e_im), (o_re, o_im) = fields
    return (e_re + o_re, e_im + o_im), (e_re - o_re, e_im - o_im)


def light(e):
    power = e[0] * e[0] + e[1] * e[1]
    return jnp.sum(power.reshape(MATES, 16, 256), axis=0)


def sensitivity(intensity, target, doses):
    total = 0.0
    for dose in doses:
        printed = jax.nn.sigmoid(steepness * (dose * intensity - threshold))
        total = total + (printed - target) * printed * (1.0 - printed) * (steepness * dose)
    return total


def cotangent(e, sens):
    spread = jnp.broadcast_to((2.0 * sens)[None], (MATES, 16, 256)).reshape(128, 256)
    return jnp.concatenate([spread * e[0], spread * e[1]], 0)


def back_columns(lo, hi, table, chunk):
    rows = slice(chunk * 256, chunk * 256 + 256)
    return dot(low(lo + hi), table[rows, : 2 * EVEN]), dot(low(lo - hi), table[rows, 2 * EVEN :])


def back_rows(parts):
    real, imag = [], []
    for part in parts:
        real.append(part[:128, :EVEN] + part[128:, EVEN:])
        imag.append(part[128:, :EVEN] - part[:128, EVEN:])
    return low(jnp.concatenate(real + imag, 1))


def grad_spectrum(got, table, h_re, h_im):
    wide = jnp.concatenate([got[s] for s in range(8)], 1).astype(jnp.float32)
    late = jnp.concatenate([got[s] for s in range(8, 16)], 1).astype(jnp.float32)
    real, imag = [], []
    for par, left in enumerate((wide + late, wide - late)):
        out = dot(low(left), table[:, par * 2 * EVEN : (par + 1) * 2 * EVEN])
        real.append(out[:32, :EVEN] + out[32:, EVEN:])
        imag.append(out[32:, :EVEN] - out[:32, EVEN:])
    g_re, g_im = jnp.concatenate(real, 1), jnp.concatenate(imag, 1)
    return low(jnp.concatenate([h_re * g_re + h_im * g_im, h_re * g_im - h_im * g_re], 0))


def adjoint_rows(d, table, roll):
    halves = []
    for par in range(2):
        left = d[:, par * EVEN : par * EVEN + EVEN]
        out = dot(left, table[par * EVEN : par * EVEN + EVEN, :])
        halves.append(
            jnp.concatenate([out[:32, :HALF] - out[32:, HALF:], out[:32, HALF:] + out[32:, :HALF]], 0)
        )
    up, down = halves[0] + halves[1], halves[0] - halves[1]
    first = lane_of((64, 128)) < 64
    blocks = []
    for m in range(8):
        u, v = up[:, 128 * m : 128 * m + 128], down[:, 128 * m : 128 * m + 128]
        blocks.append(low(jnp.where(first, u, roll(v))))
        blocks.append(low(jnp.where(first, roll(u), v)))
    return blocks


def adjoint_sum(got):
    total = jnp.sum(got.astype(jnp.float32), axis=0)
    return jnp.concatenate([total, total], 0).T


def mask_grad(got, table):
    first = lane_of((8, 128)) < 64
    wide = jnp.concatenate([jnp.where(first, got[2 * p], got[2 * p + 1]) for p in range(8)], 1)
    odd = (lane_of(wide.shape) // 16) % 2
    left = jnp.concatenate([jnp.where(odd == 0, wide, 0.0), jnp.where(odd == 0, 0.0, wide)], 0)
    out = dot(low(left), table[:, :])
    return out[:8] + out[8:], out[:8] - out[8:]


def kernel(
    mask_hbm, target_hbm, h_hbm, dose_ref, *rest
):
    table_hbm = rest[:6]
    params_out, light_out = rest[6:8]
    (
        t_in, t_own, t_to, t_from, t_toown, t_mix, h, target, acc, half,
        r0, s1, r1, s2, r2, s3, r3, s4, r4, s5, r5, s6, r6, s7, r7, s8, r8, s9, r9, s10, r10,
        local_sem, send_sem, recv_sem,
    ) = rest[8:]
    me_k, me_s = lax.axis_index("kern"), lax.axis_index("slab")
    mate, focus = me_k // 2, me_k % 2
    vmem_tables = (t_in, t_own, t_to, t_from, t_toown, t_mix)

    loads = [pltpu.make_async_copy(src, dst, local_sem.at[n]) for n, (src, dst) in enumerate(zip(table_hbm, vmem_tables))]
    own_block = pltpu.make_async_copy(mask_hbm.at[pl.ds(pl.multiple_of(8 * me_k, 8), 8)], r0.at[me_k], local_sem.at[6])
    load_h = pltpu.make_async_copy(h_hbm, h, local_sem.at[7])
    load_target = pltpu.make_async_copy(
        target_hbm.at[pl.ds(pl.multiple_of(16 * mate, 16), 16)], target, local_sem.at[8]
    )
    own_block.start()
    loads[0].start()
    loads[1].start()
    load_h.start()
    for n in range(2, 6):
        loads[n].start()
    load_target.start()

    def to_kern(t):
        return (lax.rem(me_k + t, KERNS), me_s)

    def to_slab(t):
        return (me_k, lax.rem(me_s + t, SLABS))

    barrier = pltpu.get_barrier_semaphore()

    def greet(t, carry):
        pl.semaphore_signal(barrier, inc=1, device_id=to_kern(t), device_id_type=MESH)
        pl.semaphore_signal(barrier, inc=1, device_id=to_slab(t), device_id_type=MESH)
        return carry

    lax.fori_loop(1, 16, greet, 0)
    pl.semaphore_wait(barrier, 30)

    def send(phase, src, dst, device):
        pltpu.make_async_remote_copy(
            src_ref=src, dst_ref=dst, send_sem=send_sem.at[phase], recv_sem=recv_sem.at[phase],
            device_id=device, device_id_type=MESH,
        ).start()

    sent = []

    def over_kern(phase, source, dst, size):
        def one(t, carry):
            device = to_kern(t)
            send(phase, source(device[0]), dst.at[me_k], device)
            return carry

        lax.fori_loop(1, KERNS, one, 0, unroll=True)
        sent.append((phase, size))

    def over_slab(phase, source, dst, size):
        def one(t, carry):
            device = to_slab(t)
            send(phase, source(device[1]), dst.at[me_s], device)
            return carry

        lax.fori_loop(1, SLABS, one, 0, unroll=True)
        sent.append((phase, size))

    def over_mates(phase, source, dst, size):
        def one(t, carry):
            other = lax.rem(mate + t, MATES)
            send(phase, source(other), dst.at[mate], (2 * other + focus, me_s))
            return carry

        lax.fori_loop(1, MATES, one, 0, unroll=True)
        sent.append((phase, size))

    def arrive(phase, dst):
        rest_of = dst.at[pl.ds(0, dst.shape[0] - 1)]
        pltpu.make_async_copy(rest_of, rest_of, recv_sem.at[phase]).wait()

    over_kern(0, lambda k: mask_hbm.at[pl.ds(pl.multiple_of(8 * k, 8), 8)], r0, r0)
    own_block.wait()
    arrive(0, r0)
    lo = jnp.concatenate([r0[b] for b in range(8)], 1)
    hi = jnp.concatenate([r0[b] for b in range(8, 16)], 1)

    for step in range(STEPS):
        base = 1 + 8 * step
        b1, b2, b3, b4, b5, b6, b7, b8 = (
            (s.at[step], r.at[step])
            for s, r in ((s1, r1), (s2, r2), (s3, r3), (s4, r4), (s5, r5), (s6, r6), (s7, r7), (s8, r8))
        )
        mask_lo, mask_hi = jnp.tanh(lo), jnp.tanh(hi)
        if step == 0:
            loads[0].wait()
        columns = mask_to_columns(mask_lo, mask_hi, t_in)
        for p in range(8):
            b1[0][p] = columns[:, 128 * p : 128 * p + 128]
        over_slab(base, lambda s: b1[0].at[s // 2], b1[1], b1[1])
        b1[1][me_s] = b1[0][me_s // 2]
        arrive(base, b1[1])

        half[...] = columns_transposed(b1[1][...])
        b2[0][...] = low(half[pl.ds(pl.multiple_of(64 * (me_s % 2), 64), 64), :])
        over_kern(base + 1, lambda k: b2[0], b2[1], b2[1])
        b2[1][me_k] = b2[0][...]
        if step == 0:
            loads[1].wait()
            load_h.wait()
        arrive(base + 1, b2[1])

        s_re, s_im = spectrum(b2[1], t_own)
        g = filtered(h[0], h[1], s_re, s_im)
        if step == 0:
            loads[2].wait()
        for q in range(4):
            first, second = rows_of(g, t_to, q)
            for n in range(2):
                b3[0][2 * q + n] = first[:, 128 * n : 128 * n + 128]
                b3[0][2 * q + n + 8] = second[:, 128 * n : 128 * n + 128]
        over_slab(base + 2, lambda s: b3[0].at[s], b3[1], b3[1])
        b3[1][me_s] = b3[0][me_s]
        arrive(base + 2, b3[1])

        for h8 in range(2):
            for q in range(4):
                block = b3[1][8 * h8 : 8 * h8 + 8, 16 * q : 16 * q + 16, :].reshape(128, 128)
                b4[0][:, 256 * q + 128 * h8 : 256 * q + 128 * h8 + 128] = turn(block)
        over_mates(base + 3, lambda j: b4[0].at[pl.ds(pl.multiple_of(16 * j, 16), 16)], b4[1], b4[1])
        b4[1][mate] = b4[0][pl.ds(pl.multiple_of(16 * mate, 16), 16), :]
        if step == 0:
            loads[3].wait()
            load_target.wait()
        arrive(base + 3, b4[1])

        x = b4[1][...].reshape(128, 2 * F)
        doses = [dose_ref[d] for d in range(2)]
        for q in range(4):
            cots = []
            for n, e in enumerate(field(x, t_to, q)):
                intensity = light(e)
                start = n * HALF + 256 * q
                if step == STEPS - 1:
                    for m in range(2):
                        s9[start // 128 + m] = low(intensity[:, 128 * m : 128 * m + 128])
                sens = sensitivity(intensity, target[:, start : start + 256].astype(jnp.float32), doses)
                cots.append(cotangent(e, sens))
            for par, term in enumerate(back_columns(cots[0], cots[1], t_from, q)):
                if q == 0:
                    acc[par] = term
                else:
                    acc[par] += term
        b5[0][...] = back_rows((acc[0], acc[1])).reshape(MATES, 16, 2 * F)
        over_mates(base + 4, lambda j: b5[0].at[j], b5[1], b5[1])
        b5[1][mate] = b5[0][mate]
        if step == STEPS - 1:
            over_kern(17, lambda k: s9.at[k], r9, r9)
            r9[me_k] = s9[me_k]
        arrive(base + 4, b5[1])

        for h8 in range(2):
            for q in range(4):
                block = b5[1][:, :, 256 * q + 128 * h8 : 256 * q + 128 * h8 + 128].reshape(128, 128)
                b6[0][8 * h8 : 8 * h8 + 8, 16 * q : 16 * q + 16, :] = turn(block).reshape(8, 16, 128)
        over_slab(base + 5, lambda s: b6[0].at[s], b6[1], b6[1])
        b6[1][me_s] = b6[0][me_s]
        arrive(base + 5, b6[1])

        d = grad_spectrum(b6[1], t_from, h[0], h[1])
        if step == 0:
            loads[4].wait()
        for n, block in enumerate(adjoint_rows(d, t_toown, lambda v: pltpu.roll(v, 64, 1))):
            b7[0][n] = block
        over_kern(base + 6, lambda k: b7[0].at[k], b7[1], b7[1])
        b7[1][me_k] = b7[0][me_k]
        arrive(base + 6, b7[1])

        b8[0][...] = adjoint_sum(b7[1][...]).reshape(SLABS, 8, 128)
        over_slab(base + 7, lambda s: b8[0].at[s], b8[1], b8[1])
        b8[1][me_s] = b8[0][me_s]
        if step == 0:
            loads[5].wait()
        arrive(base + 7, b8[1])

        grad_lo, grad_hi = mask_grad(b8[1], t_mix)
        lo = lo - step_rate * grad_lo * (1.0 - mask_lo * mask_lo)
        hi = hi - step_rate * grad_hi * (1.0 - mask_hi * mask_hi)

    for b in range(8):
        s10[b] = lo[:, 128 * b : 128 * b + 128]
        s10[b + 8] = hi[:, 128 * b : 128 * b + 128]
    over_kern(18, lambda k: s10.at[k], r10, r10)
    r10[me_k] = s10[me_k]
    arrive(17, r9)
    for k in range(KERNS):
        light_out[k % 2, 16 * (k // 2) : 16 * (k // 2) + 16, :] = r9[k].astype(jnp.float32)
    arrive(18, r10)
    params_out[...] = r10[...].reshape(128, 128)
    for phase, buffer in sent:
        rest_of = buffer.at[pl.ds(0, buffer.shape[0] - 1)]
        pltpu.make_async_copy(rest_of, rest_of, send_sem.at[phase]).wait()


def body(mask_params, target_bits, kernels, weights, dose_factors):
    scaled = kernels[0] * jnp.sqrt(weights[0])
    h = scaled.reshape(2, EVEN, 2, 16, 2).transpose(0, 4, 3, 2, 1).reshape(2, 32, F)
    f32, bf16 = jnp.float32, jnp.bfloat16
    consts = [jnp.asarray(t) for t in tables()]
    exchange = []
    for shape, send_shape, kind in (
        ((16, 8, 128), (8, 8, 128), f32),
        ((16, 64, 128), (64, 128), bf16),
        ((16, 64, 128), (16, 64, 128), bf16),
        ((8, 16, 1024), (128, 1024), bf16),
        ((8, 16, 1024), (8, 16, 1024), bf16),
        ((16, 64, 128), (16, 64, 128), bf16),
        ((16, 64, 128), (16, 64, 128), bf16),
        ((16, 8, 128), (16, 8, 128), f32),
    ):
        exchange += [pltpu.VMEM((STEPS,) + send_shape, kind), pltpu.VMEM((STEPS,) + shape, kind)]
    hbm, vmem = pl.BlockSpec(memory_space=pl.ANY), pl.BlockSpec(memory_space=pltpu.VMEM)
    params, intensity = pl.pallas_call(
        kernel,
        out_shape=(jax.ShapeDtypeStruct((128, 128), f32), jax.ShapeDtypeStruct((2, 128, 128), f32)),
        in_specs=[hbm, hbm, hbm, pl.BlockSpec(memory_space=pltpu.SMEM)] + [hbm] * 6,
        out_specs=(vmem, vmem),
        scratch_shapes=[pltpu.VMEM(t.shape, bf16) for t in consts]
        + [
            pltpu.VMEM((2, 32, F), f32),
            pltpu.VMEM((16, N), jnp.int32),
            pltpu.VMEM((2, 256, 2 * EVEN), f32),
            pltpu.VMEM((128, 128), f32),
            pltpu.VMEM((16, 8, 128), f32),
        ]
        + exchange
        + [
            pltpu.VMEM((16, 16, 128), bf16),
            pltpu.VMEM((16, 16, 128), bf16),
            pltpu.VMEM((16, 8, 128), f32),
            pltpu.VMEM((16, 8, 128), f32),
            pltpu.SemaphoreType.DMA((9,)),
            pltpu.SemaphoreType.DMA((19,)),
            pltpu.SemaphoreType.DMA((19,)),
        ],
        compiler_params=pltpu.CompilerParams(
            collective_id=0, has_side_effects=True, vmem_limit_bytes=48 * 1024 * 1024
        ),
    )(mask_params, target_bits, h, dose_factors, *consts)
    printed = jax.nn.sigmoid(
        steepness * (dose_factors[None, :, None, None] * intensity[:, None] - threshold)
    )
    return params, printed


def solution(mesh):
    in_specs = (P("slab", "kern"), P("slab", None), P("kern", None, None, "slab"), P("kern"), P())
    out_specs = (P("slab", "kern"), P(None, None, "slab", "kern"))
    return jax.shard_map(body, mesh=mesh, in_specs=in_specs, out_specs=out_specs, check_vma=False)
```

time: 1620 us -> 154 us (0.10)
  waiting for transfers between devices: 1240 us -> 0 us
  matrix products: 211 us -> 0 us
  Pallas kernels: 0 us -> 133 us
  other arithmetic: 47.4 us -> 1.77 us
  blocking collectives: 44.3 us -> 0 us
  local copies, waits for them, and re-layouts: 47.1 us -> 17.5 us
    unnamed x18 -> x0, waiting for transfers between devices: 756 us -> none
    psum x2 -> x0, waiting for transfers between devices: 244 us -> none  [body(): lax.psum(intensity_terms.astype(jnp.bfloat16), 'kern').astype(jnp.float32)]
    all_gather x4 -> x0, waiting for transfers between devices: 243 us -> none  [the longest x2 122 us: body(): cot_full = lax.all_gather(spec_cotangent, 'slab', axis=2, tiled=True)]
    dot_general x30 -> x0, matrix products: 211 us -> none  [the longest x16 132 us: plain_product(): return jnp.dot(left, right, preferred_element_type=jnp.float32)]
    pallas_call x0 -> x1, Pallas kernels: none -> 133 us  [body(): pl.pallas_call(kernel, out_shape=(jax.ShapeDtypeStruct((128, 128), f32),...]
    all_gather x2 -> x0, blocking collectives: 44.3 us -> none  [body(): lax.all_gather(mask_values.astype(jnp.bfloat16), 'kern', axis=1, tiled=True)]
    convert_element_type x13 -> x0, other arithmetic: 30.8 us -> none  [the longest x1 18.8 us: tables(): (jnp.cos(angles) * scale).astype(jnp.bfloat16)]
    unnamed x35 -> x11, local copies, waits for them, and re-layouts: 22.5 us -> 2.23 us
  transfers between devices with their start and end apart: 12 -> 0, of which waited for: 12 -> 0; matrix products, arithmetic and copies ran while one was open for 0% -> 0% of each run, Pallas kernels for 0% -> 0%
where the time goes in v1:
time: 154 us; the launch traced here: 153 us
  Pallas kernels  133 us (86%)
  local copies, waits for them, and re-layouts  17.5 us (11%)
  other arithmetic  1.77 us (1%)
    pallas_call x1, Pallas kernels, body(): pl.pallas_call(kernel, out_shape=(jax.ShapeDtypeStruct((128, 128), f32),...  133 us
    mul x1, local copies, waits for them, and re-layouts, body(): scaled = kernels[0] * jnp.sqrt(weights[0])  9.75 us
    transpose x1, local copies, waits for them, and re-layouts, body(): scaled.reshape(2, EVEN, 2, 16, 2).transpose(0, 4, 3, 2, 1).reshape(2, 32, F)  5.38 us

profile of v1, /device:TPU:1, one launch (start us, length us, event | category | flops | bytes accessed | tf_op | source)
XLA Modules:
  0.0 153.4 jit_solution(2459272113097467102)
XLA Ops:
  1.3 0.9 broadcast_multiply_fusion
  2.2 9.8 %mul.31 = f32[2,256,2,16,2]{2,1,4,3,0:T(8,128)} reshape(f32[1,2,512,32]{2,3,1,0:T(8,128)S(1)} %broadcast_multiply_fusion) | data formatting | bytes 262144 | tf_op jit(solution)/shard_map/mul | solution.py:402
  12.0 0.0 copy-start
  12.0 0.0 copy-start.2
  12.0 0.0 copy-start.3
  12.0 0.0 copy-start.4
  12.0 5.4 %copy.14 = f32[2,2,16,2,256]{4,3,2,1,0:T(2,128)S(1)} copy(f32[2,2,16,2,256]{3,4,1,2,0:T(8,128)} %bitcast.6) | data formatting | bytes 262144 | tf_op jit(solution)/shard_map/transpose | solution.py:403
  17.4 0.1 reshape.14.h_hbm
  17.5 0.0 copy-done
  17.5 0.0 copy-done.2
  17.5 0.0 copy-done.3
  17.5 0.0 copy-done.4
  17.5 0.0 copy-start.1
  17.6 1.6 %copy-done.1 = bf16[1024,1024]{1,0:T(8,128)(2,1)S(1)} copy-done((bf16[1024,1024]{1,0:T(8,128)(2,1)S(1)}, bf16[1024,1024]{1,0:T(8,128)(2,1)}, u32[]{:S(2)}) %copy-start.1) | copy-done | bytes 2097176
  19.1 132.8 %shard_map.122 = (f32[128,128]{1,0:T(8,128)S(1)}, f32[2,128,128]{2,1,0:T(8,128)S(1)}) custom-call(f32[128,128]{1,0:T(8,128)S(1)} %copy-done.3, s32[128,2048]{1,0:T(8,128)S(1)} %copy-done.2, f32[2,32,512]{2,1,0:T(8,128)S(1)} %reshape.14.h_hbm, f32[2]{0:T(128)S(1)} %copy-done.4, bf16[1024,1024]{1,0:T(8,128)(2,1)S(1)} %copy-done.1, ...), custom_call_target="tpu_custom_call" | custom-call | tf_op jit(solution)/shard_map/pallas_call | solution.py:419
  151.9 0.8 add_divide_fusion
  152.8 0.6 copy.17
Async XLA Ops:
  12.0 5.5 %copy-start = (bf16[2048,512]{1,0:T(8,128)(2,1)S(1)}, bf16[2048,512]{1,0:T(8,128)(2,1)}, u32[]{:S(2)}) copy-start(bf16[2048,512]{1,0:T(8,128)(2,1)} %constant.19.clone.rest_1_) | copy-start | bytes 6291460
  12.0 5.5 %copy-start.2 = (s32[128,2048]{1,0:T(8,128)S(1)}, s32[128,2048]{1,0:T(8,128)}, u32[]{:S(2)}) copy-start(s32[128,2048]{1,0:T(8,128)} %target_hbm.1) | copy-start | bytes 3145732
  12.0 5.5 %copy-start.3 = (f32[128,128]{1,0:T(8,128)S(1)}, f32[128,128]{1,0:T(8,128)}, u32[]{:S(2)}) copy-start(f32[128,128]{1,0:T(8,128)} %mask_hbm.1) | copy-start | bytes 196612
  12.0 5.5 %copy-start.4 = (f32[2]{0:T(128)S(1)}, f32[2]{0:T(128)}, u32[]{:S(2)}) copy-start(f32[2]{0:T(128)} %dose_ref.1) | copy-start | bytes 28
  17.5 1.6 %copy-start.1 = (bf16[1024,1024]{1,0:T(8,128)(2,1)S(1)}, bf16[1024,1024]{1,0:T(8,128)(2,1)}, u32[]{:S(2)}) copy-start(bf16[1024,1024]{1,0:T(8,128)(2,1)} %constant.18.clone.rest_0_) | copy-start | bytes 6291460

commit v2 on v0

v2 whole, which is shorter than its diff:
```python
import math

import jax
import jax.numpy as jnp
import ml_dtypes
import numpy as np
from jax import lax
from jax.experimental import pallas as pl
from jax.experimental.pallas import tpu as pltpu
from jax.sharding import PartitionSpec as P

N = 2048
F = 512
STEPS = 2
HALF = N // 2
EVEN = F // 2
KERNS = 16
SLABS = 16
PEERS = 64

steepness = 3.0
threshold = 1.0
step_rate = 0.4
MESH = pl.DeviceIdType.MESH


def tables():
    index = np.concatenate([np.arange(0, F, 2), np.arange(1, F, 2)])
    phases = ((index[:, None] - F // 2) * np.arange(HALF)[None, :]) % N
    angles = phases * (2.0 * math.pi / N)
    scale = 1.0 / math.sqrt(N)
    cos, sin = np.cos(angles) * scale, np.sin(angles) * scale
    y, p, k, i = np.meshgrid(np.arange(2), np.arange(2), np.arange(8), np.arange(16), indexing="ij")
    rows = [((y * 4 + 2 * h + p) * 128 + k * 16 + i).reshape(-1) for h in range(2)]
    to_freq = np.stack([np.concatenate([cos[:, r], sin[:, r]], 1) for r in rows])
    to_rows = to_freq.reshape(2, 2, EVEN, 2, 512).transpose(0, 4, 1, 3, 2).reshape(2, 512, HALF)
    to_cols = np.concatenate([cos, sin], 1)
    from_cols = np.concatenate([cos[:EVEN].T, sin[:EVEN].T, cos[EVEN:].T, sin[EVEN:].T], 1)
    c, s = cos.reshape(2, 4, 64, HALF), sin.reshape(2, 4, 64, HALF)
    mixed = np.stack([c, -s], 2).reshape(2, F, HALF)
    cast = lambda table: np.ascontiguousarray(table).astype(np.float32).astype(ml_dtypes.bfloat16)
    return [cast(t) for t in (mixed.transpose(0, 2, 1), to_freq, to_rows, to_cols, from_cols, mixed)]


def dot(left, right):
    return jnp.dot(left, right, preferred_element_type=jnp.float32)


def low(value):
    return value.astype(jnp.bfloat16)


def wide(value):
    return value.astype(jnp.float32)


def is_real(shape):
    return lax.broadcasted_iota(jnp.int32, shape, len(shape) - 1) < 64


def to_spectrum(got, table, roll):
    lo, hi = wide(got[:512]), wide(got[512:])
    parts = []
    for par, x in enumerate((lo + hi, lo - hi)):
        turned = jnp.where(is_real(x.shape), roll(x), -roll(x))
        both = low(jnp.concatenate([x, turned], 0))
        parts.append(dot(table[par * EVEN : par * EVEN + EVEN, :], both))
    return jnp.concatenate(parts, 0)


def to_pixel_rows(spec, table, roll):
    turned = jnp.where(is_real(spec.shape), -roll(spec), roll(spec))
    parts = []
    for par in range(2):
        rows = slice(par * EVEN, par * EVEN + EVEN)
        both = low(jnp.concatenate([spec[rows], turned[rows]], 0))
        parts.append(dot(table[:, par * F : par * F + F], both))
    return low(parts[0] + parts[1]), low(parts[0] - parts[1])


def pair_in(first, second, roll):
    first, second = wide(first), wide(second)
    real = is_real(first.shape)
    return low(jnp.where(real, first, roll(second))), low(jnp.where(real, roll(first), second))


def pair_out(re, im, roll):
    real = is_real(re.shape)
    return low(jnp.where(real, re, roll(im))), low(jnp.where(real, roll(re), im))


def field(lefts, table, chunk):
    fields = []
    for par, left in enumerate(lefts):
        rows = slice(par * EVEN, par * EVEN + EVEN)
        with_cos = dot(left, table[rows, chunk * 256 : chunk * 256 + 256])
        with_sin = dot(left, table[rows, HALF + chunk * 256 : HALF + chunk * 256 + 256])
        fields.append((with_cos[:128] - with_sin[128:], with_cos[128:] + with_sin[:128]))
    (e_re, e_im), (o_re, o_im) = fields
    return (e_re + o_re, e_im + o_im), (e_re - o_re, e_im - o_im)


def light(e):
    power = e[0] * e[0] + e[1] * e[1]
    return jnp.sum(power.reshape(8, 16, 256), axis=0)


def sensitivity(intensity, target, doses):
    total = 0.0
    for dose in doses:
        printed = jax.nn.sigmoid(steepness * (dose * intensity - threshold))
        total = total + (printed - target) * printed * (1.0 - printed) * (steepness * dose)
    return total


def cotangent(e, sens):
    spread = jnp.broadcast_to((2.0 * sens)[None], (8, 16, 256)).reshape(128, 256)
    return jnp.concatenate([spread * e[0], spread * e[1]], 0)


def back_columns(lo, hi, table, chunk):
    rows = slice(chunk * 256, chunk * 256 + 256)
    return dot(low(lo + hi), table[rows, :F]), dot(low(lo - hi), table[rows, F:])


def back_tiles(part, roll):
    re = part[:128, :EVEN] + part[128:, EVEN:]
    im = part[128:, :EVEN] - part[:128, EVEN:]
    tiles = []
    for m in range(2):
        lanes = slice(128 * m, 128 * m + 128)
        tiles.extend(pair_out(re[:, lanes], im[:, lanes], roll))
    return tiles


def grad_part(got, table):
    blocks = jnp.sum(wide(got).reshape(2, 4, 8, 16, 128), axis=(0, 2))
    return dot(low(jnp.concatenate([blocks[y] for y in range(4)], 1)), table[:, :])


def kernel(mask_hbm, target_hbm, h_hbm, weight_ref, dose_ref, *rest):
    table_hbm = rest[:6]
    params_out, light_out = rest[6:8]
    (
        t_mask, t_freq, t_rows, t_cols, t_back, t_mix,
        h_raw, h_re, h_im, h_turn, target_raw, target, acc,
        r0, hs, hr, ts, tr, s9, r9, s10, r10,
        s_a, r_a, s_sp, r_sp, s_b, r_b, s_db, r_db, s_d, r_d, s_da, r_da, s_g, r_g,
        local_sem, send_sem, recv_sem,
    ) = rest[8:]
    me_k, me_s = lax.axis_index("kern"), lax.axis_index("slab")
    kappa, core = me_k // 2, me_k % 2
    z_lo, x_at = kappa // 4, kappa % 4
    y_at, focus, par = me_s // 4, (me_s % 4) // 2, me_s % 2
    place = y_at * 16 + par * 8 + kappa
    sign = (1 - 2 * core).astype(jnp.float32)
    roll = lambda v: pltpu.roll(v, 64, 1)

    def device(kappa, core, y, focus, par):
        return (2 * kappa + core, 4 * y + 2 * focus + par)

    sibling = (me_k + 1 - 2 * core, me_s)

    own_block = pltpu.make_async_copy(
        mask_hbm.at[pl.ds(pl.multiple_of(16 * kappa, 16), 16)], r0.at[me_k], local_sem.at[6]
    )
    load_target = pltpu.make_async_copy(
        target_hbm.at[pl.ds(pl.multiple_of(16 * kappa, 16), 16)], target_raw, local_sem.at[8]
    )
    loads = [
        pltpu.make_async_copy(table_hbm[0].at[core], t_mask, local_sem.at[0]),
        pltpu.make_async_copy(table_hbm[1].at[core], t_freq, local_sem.at[1]),
        pltpu.make_async_copy(table_hbm[2].at[core], t_rows, local_sem.at[2]),
        pltpu.make_async_copy(table_hbm[3], t_cols, local_sem.at[3]),
        pltpu.make_async_copy(table_hbm[4], t_back, local_sem.at[4]),
        pltpu.make_async_copy(table_hbm[5].at[core], t_mix, local_sem.at[5]),
    ]
    own_block.start()
    for b in range(4):
        pltpu.make_async_copy(h_hbm.at[:, :, pl.ds(128 * b, 128)], h_raw.at[b], local_sem.at[7]).start()
    load_target.start()
    for load in loads:
        load.start()

    barrier = pltpu.get_barrier_semaphore()

    def greet(t, carry):
        slab = lax.rem(me_s + t, SLABS)
        kern = lax.rem(me_k + t, KERNS)
        pl.semaphore_signal(barrier, inc=1, device_id=(me_k, slab), device_id_type=MESH)
        pl.semaphore_signal(barrier, inc=1, device_id=(kern, me_s), device_id_type=MESH)
        return carry

    lax.fori_loop(1, 16, greet, 0)

    pltpu.make_async_copy(h_raw, h_raw, local_sem.at[7]).wait()
    root = jnp.sqrt(jnp.full((16, 128), weight_ref[0], jnp.float32))
    for q in range(2):
        for part in range(2):
            for b in range(4):
                own_rows = h_raw[b, part, pl.ds(q, 16, stride=2), :]
                hs[q, 16 * part : 16 * part + 16, 128 * b : 128 * b + 128] = low(own_rows * root)
    load_target.wait()
    ts[...] = low(wide(target_raw[...]))

    pl.semaphore_wait(barrier, 30)

    sent = []

    def send(phase, src, dst, where):
        pltpu.make_async_remote_copy(
            src_ref=src, dst_ref=dst, send_sem=send_sem.at[phase], recv_sem=recv_sem.at[phase],
            device_id=where, device_id_type=MESH,
        ).start()

    def maybe_own(phase, src, dst, where, is_own):
        if is_own is True:
            pltpu.make_async_copy(src, dst, recv_sem.at[phase]).start()
            return

        @pl.when(is_own)
        def _():
            pltpu.make_async_copy(src, dst, recv_sem.at[phase]).start()

        @pl.when(jnp.logical_not(is_own))
        def _():
            send(phase, src, dst, where)

    def sent_maybe(phase, buffer, is_own):
        @pl.when(jnp.logical_not(is_own))
        def _():
            pltpu.make_async_copy(buffer, buffer, send_sem.at[phase]).wait()

    def take(phase, buffer):
        pltpu.make_async_copy(buffer, buffer, recv_sem.at[phase]).wait()

    def given(phase, buffer):
        pltpu.make_async_copy(buffer, buffer, send_sem.at[phase]).wait()

    def direct(phase, copy, dst, is_own):
        for dx in (2, 1, 3, 0):
            for dy in (2, 1, 3, 0):
                for db, dz in ((1, 1), (1, 0), (0, 1), (0, 0)):
                    to_kappa = lax.rem(z_lo + dz, 2) * 4 + lax.rem(x_at + dx, 4)
                    src, where = copy(to_kappa, lax.rem(y_at + dy, 4), db)
                    if (dx, dy, db, dz) == (0, 0, 0, 0):
                        maybe_own(phase, src, dst, where, is_own)
                    else:
                        send(phase, src, dst, where)
        sent.append((phase, is_own))

    def out_rows(t, carry):
        kern = lax.rem(me_k + t, KERNS)
        send(0, mask_hbm.at[pl.ds(pl.multiple_of(16 * (kern // 2), 16), 16)], r0.at[me_k], (kern, me_s))
        return carry

    lax.fori_loop(1, KERNS, out_rows, 0, unroll=True)
    own_block.wait()
    take(0, r0.at[pl.ds(0, KERNS - 1)])
    lo = jnp.concatenate([r0[b] for b in range(8)], 1)
    hi = jnp.concatenate([r0[b] for b in range(8, 16)], 1)

    own_target = focus == core
    for step in range(STEPS):
        base = 5 + 7 * step
        first, last = step == 0, step == STEPS - 1

        mask_lo, mask_hi = jnp.tanh(lo), jnp.tanh(hi)
        if first:
            loads[0].wait()
        columns = dot(low(mask_lo + sign * mask_hi), t_mask[...])
        for b in range(4):
            s_a[step, b] = low(columns[:, 128 * b : 128 * b + 128])
        direct(
            base,
            lambda k, y, b: (s_a.at[step, y], device(k, focus, y, lax.rem(focus + b, 2), core)),
            r_a.at[step, place],
            (par == core) & (focus == core),
        )
        if first:
            for q in range(2):
                for to_core in range(2):
                    maybe_own(
                        1, hs.at[q], hr.at[me_s % 4], device(kappa, to_core, y_at, core, q),
                        (me_s % 4 == 2 * core + q) & (core == to_core),
                    )

            @pl.when(own_target)
            def _():
                send(2, ts, tr, device(kappa, core, y_at, 1 - focus, par))

            loads[1].wait()
        take(base, r_a.at[step])
        part = to_spectrum(r_a[step].reshape(HALF, 128), t_freq, roll)
        s_sp[step] = low(part)
        send(base + 1, s_sp.at[step], r_sp.at[step], sibling)
        if first:
            take(1, hr)
            flat = jnp.concatenate(
                [hr[z, 16 * c : 16 * c + 16, :] for c in range(2) for z in range(4)], 0
            )
            h_turn[...] = wide(flat).T
            for q in range(2):
                rows = slice(q * EVEN, q * EVEN + EVEN)
                h = h_turn[pl.ds(q, EVEN, stride=2), :]
                turned = roll(h)
                h_re[rows, :] = jnp.where(is_real(h.shape), h, turned)
                h_im[rows, :] = jnp.where(is_real(h.shape), -turned, h)
            loads[2].wait()
        take(base + 1, r_sp.at[step])
        spec = part + wide(r_sp[step])

        filtered = h_re[...] * spec + h_im[...] * roll(spec)
        low_rows, high_rows = to_pixel_rows(filtered, t_rows, roll)
        s_b[step, :32] = low_rows.reshape(32, 16, 128)
        s_b[step, 32:] = high_rows.reshape(32, 16, 128)

        def to_place(k, y, b):
            to_par = lax.rem(par + b, 2)
            return y * 16 + to_par * 8 + k, to_par

        def rows_out(k, y, b):
            at, to_par = to_place(k, y, b)
            return s_b.at[step, at], device(k, core, y, focus, to_par)

        direct(base + 2, rows_out, r_b.at[step, par * 32 + y_at * 8 + kappa], True)
        if first:
            loads[3].wait()
            loads[4].wait()

            @pl.when(own_target)
            def _():
                target[...] = ts[...]

            @pl.when(jnp.logical_not(own_target))
            def _():
                take(2, tr)
                target[...] = tr[...]
        take(base + 2, r_b.at[step])

        lefts = []
        for q in range(2):
            re, im = [], []
            for m in range(2):
                at = 32 * q + 16 * m
                a, b = pair_in(r_b[step, at : at + 8].reshape(128, 128), r_b[step, at + 8 : at + 16].reshape(128, 128), roll)
                re.append(a)
                im.append(b)
            lefts.append(jnp.concatenate([jnp.concatenate(re, 1), jnp.concatenate(im, 1)], 0))
        doses = [dose_ref[d] for d in range(2)]
        for chunk in range(4):
            cots = []
            for n, e in enumerate(field(lefts, t_cols, chunk)):
                intensity = light(e)
                start = n * HALF + 256 * chunk
                if last:
                    for m in range(2):
                        s9[start // 128 + m] = low(intensity[:, 128 * m : 128 * m + 128])
                sens = sensitivity(intensity, wide(target[:, start : start + 256]), doses)
                cots.append(cotangent(e, sens))
            for q, term in enumerate(back_columns(cots[0], cots[1], t_back, chunk)):
                if chunk == 0:
                    acc[q] = term
                else:
                    acc[q] += term
        for q in range(2):
            for y, tile in enumerate(back_tiles(acc[q], roll)):
                at = 32 * q + 8 * y
                s_db[step, at : at + 8] = tile.reshape(8, 16, 128)

        def back_out(k, y, b):
            to_par = lax.rem(par + b, 2)
            return s_db.at[step, to_par * 32 + y * 8 + k], device(k, core, y, focus, to_par)

        direct(base + 3, back_out, r_db.at[step, place], True)
        if last:
            home = 4 * y_at + 2 * core + par
            maybe_own(3, s9.at[me_k], r9.at[focus * 8 + kappa], (me_k, home), own_target)

            def light_home(t, carry):
                kern = lax.rem(me_k + t, KERNS)
                send(3, s9.at[kern], r9.at[focus * 8 + kappa], (kern, home))
                return carry

            lax.fori_loop(1, KERNS, light_home, 0, unroll=True)
        take(base + 3, r_db.at[step])

        g = to_spectrum(r_db[step].reshape(HALF, 128), t_freq, roll)
        part = h_re[...] * g - h_im[...] * roll(g)
        s_d[step] = low(part)
        send(base + 4, s_d.at[step], r_d.at[step], sibling)
        take(base + 4, r_d.at[step])
        low_rows, high_rows = to_pixel_rows(part + wide(r_d[step]), t_rows, roll)
        s_da[step, :32] = low_rows.reshape(32, 16, 128)
        s_da[step, 32:] = high_rows.reshape(32, 16, 128)

        def adjoint_out(k, y, b):
            at, to_par = to_place(k, y, b)
            return s_da.at[step, at], device(k, par, y, core, to_par)

        direct(
            base + 5, adjoint_out, r_da.at[step, focus * 32 + y_at * 8 + kappa], (par == core) & (focus == core)
        )
        if first:
            loads[5].wait()
        take(base + 5, r_da.at[step])

        own = grad_part(r_da[step], t_mix)
        s_g[step] = own
        send(base + 6, s_g.at[step], r_g.at[step], sibling)
        take(base + 6, r_g.at[step])
        other = r_g[step]
        lo = lo - step_rate * (own + other) * (1.0 - mask_lo * mask_lo)
        hi = hi - step_rate * (sign * (own - other)) * (1.0 - mask_hi * mask_hi)

    for b in range(8):
        s10[b] = lo[:, 128 * b : 128 * b + 128]
        s10[b + 8] = hi[:, 128 * b : 128 * b + 128]
    at_home = me_k // 8 == core
    kern = 8 * core + me_k % 8
    maybe_own(4, s10.at[kern], r10.at[kappa], (kern, me_s), at_home)

    def params_home(t, carry):
        kern = 8 * core + lax.rem(me_k + t, 8)
        send(4, s10.at[kern], r10.at[kappa], (kern, me_s))
        return carry

    lax.fori_loop(1, 8, params_home, 0, unroll=True)
    take(3, r9)
    for k in range(KERNS):
        light_out[k // 8, 16 * (k % 8) : 16 * (k % 8) + 16, :] = wide(r9[k])
    take(4, r10)
    params_out[...] = r10[...].reshape(128, 128)

    given(0, r0.at[pl.ds(0, KERNS - 1)])
    for q in range(2):
        for to_core in range(2):
            sent_maybe(1, hs.at[q], (me_s % 4 == 2 * core + q) & (core == to_core))
    sent_maybe(2, ts, jnp.logical_not(own_target))
    given(3, s9.at[pl.ds(0, KERNS - 1)])
    sent_maybe(3, s9.at[0], own_target)
    given(4, s10.at[pl.ds(0, 7)])
    sent_maybe(4, s10.at[0], at_home)
    for phase, is_own in sent:
        given(phase, r_b.at[0, pl.ds(0, PEERS - 1)])
        if is_own is not True:
            sent_maybe(phase, r_b.at[0, 0], is_own)
    for step in range(STEPS):
        given(5 + 7 * step + 1, s_sp.at[step])
        given(5 + 7 * step + 4, s_d.at[step])
        given(5 + 7 * step + 6, s_g.at[step])


def body(mask_params, target_bits, kernels, weights, dose_factors):
    f32, bf16 = jnp.float32, jnp.bfloat16
    consts = [jnp.asarray(t) for t in tables()]
    hbm, vmem = pl.BlockSpec(memory_space=pl.ANY), pl.BlockSpec(memory_space=pltpu.VMEM)
    smem = pl.BlockSpec(memory_space=pltpu.SMEM)
    exchange = []
    for shape, send_shape, kind in (
        ((PEERS, 16, 128), (4, 16, 128), bf16),
        ((F, 128), (F, 128), bf16),
        ((PEERS, 16, 128), (PEERS, 16, 128), bf16),
        ((PEERS, 16, 128), (PEERS, 16, 128), bf16),
        ((F, 128), (F, 128), bf16),
        ((PEERS, 16, 128), (PEERS, 16, 128), bf16),
        ((16, HALF), (16, HALF), f32),
    ):
        exchange += [pltpu.VMEM((STEPS,) + send_shape, kind), pltpu.VMEM((STEPS,) + shape, kind)]
    params, intensity = pl.pallas_call(
        kernel,
        out_shape=(jax.ShapeDtypeStruct((128, 128), f32), jax.ShapeDtypeStruct((2, 128, 128), f32)),
        in_specs=[hbm, hbm, hbm, smem, smem] + [hbm] * 6,
        out_specs=(vmem, vmem),
        scratch_shapes=[
            pltpu.VMEM((HALF, F), bf16),
            pltpu.VMEM((F, HALF), bf16),
            pltpu.VMEM((F, HALF), bf16),
            pltpu.VMEM((F, N), bf16),
            pltpu.VMEM((HALF, HALF), bf16),
            pltpu.VMEM((F, HALF), bf16),
            pltpu.VMEM((4, 2, 32, 128), f32),
            pltpu.VMEM((F, 128), f32),
            pltpu.VMEM((F, 128), f32),
            pltpu.VMEM((F, 128), f32),
            pltpu.VMEM((16, N), jnp.int32),
            pltpu.VMEM((16, N), bf16),
            pltpu.VMEM((2, 256, F), f32),
            pltpu.VMEM((16, 16, 128), f32),
            pltpu.VMEM((2, 32, F), bf16),
            pltpu.VMEM((4, 32, F), bf16),
            pltpu.VMEM((16, N), bf16),
            pltpu.VMEM((16, N), bf16),
            pltpu.VMEM((16, 16, 128), bf16),
            pltpu.VMEM((16, 16, 128), bf16),
            pltpu.VMEM((16, 16, 128), f32),
            pltpu.VMEM((8, 16, 128), f32),
        ]
        + exchange
        + [
            pltpu.SemaphoreType.DMA((9,)),
            pltpu.SemaphoreType.DMA((19,)),
            pltpu.SemaphoreType.DMA((19,)),
        ],
        compiler_params=pltpu.CompilerParams(
            collective_id=0, has_side_effects=True, vmem_limit_bytes=48 * 1024 * 1024
        ),
    )(mask_params, target_bits, kernels[0].transpose(0, 2, 1), weights, dose_factors, *consts)
    printed = jax.nn.sigmoid(
        steepness * (dose_factors[None, :, None, None] * intensity[:, None] - threshold)
    )
    return params, printed


def solution(mesh):
    in_specs = (P("slab", "kern"), P("slab", None), P("kern", None, None, "slab"), P("kern"), P())
    out_specs = (P("slab", "kern"), P(None, None, "slab", "kern"))
    return jax.shard_map(body, mesh=mesh, in_specs=in_specs, out_specs=out_specs, check_vma=False)
```

time: 1620 us -> 122 us (0.08)
  waiting for transfers between devices: 1240 us -> 0 us
  matrix products: 211 us -> 0 us
  Pallas kernels: 0 us -> 112 us
  other arithmetic: 47.4 us -> 0.85 us
  blocking collectives: 44.3 us -> 0 us
  local copies, waits for them, and re-layouts: 47.1 us -> 7.43 us
    unnamed x18 -> x0, waiting for transfers between devices: 756 us -> none
    psum x2 -> x0, waiting for transfers between devices: 244 us -> none  [body(): lax.psum(intensity_terms.astype(jnp.bfloat16), 'kern').astype(jnp.float32)]
    all_gather x4 -> x0, waiting for transfers between devices: 243 us -> none  [the longest x2 122 us: body(): cot_full = lax.all_gather(spec_cotangent, 'slab', axis=2, tiled=True)]
    dot_general x30 -> x0, matrix products: 211 us -> none  [the longest x16 132 us: plain_product(): return jnp.dot(left, right, preferred_element_type=jnp.float32)]
    pallas_call x0 -> x1, Pallas kernels: none -> 112 us  [body(): pl.pallas_call(kernel, out_shape=(jax.ShapeDtypeStruct((128, 128), f32),...]
    all_gather x2 -> x0, blocking collectives: 44.3 us -> none  [body(): lax.all_gather(mask_values.astype(jnp.bfloat16), 'kern', axis=1, tiled=True)]
    convert_element_type x13 -> x0, other arithmetic: 30.8 us -> none  [the longest x1 18.8 us: tables(): (jnp.cos(angles) * scale).astype(jnp.bfloat16)]
  transfers between devices with their start and end apart: 12 -> 0, of which waited for: 12 -> 0; matrix products, arithmetic and copies ran while one was open for 0% -> 0% of each run, Pallas kernels for 0% -> 0%
where the time goes in v2:
time: 122 us; the launch traced here: 121 us
  Pallas kernels  112 us (92%)
  local copies, waits for them, and re-layouts  7.43 us (6%)
  between operations  1.3 us (1%)
    pallas_call x1, Pallas kernels, body(): pl.pallas_call(kernel, out_shape=(jax.ShapeDtypeStruct((128, 128), f32),...  112 us
    unnamed x13, local copies, waits for them, and re-layouts  7.43 us

profile of v2, /device:TPU:1, one launch (start us, length us, event | category | flops | bytes accessed | tf_op | source)
XLA Modules:
  0.0 121.4 jit_solution(18410199529952935031)
XLA Ops:
  1.3 0.0 copy-start
  1.3 1.6 %copy-done = bf16[2,512,1024]{2,1,0:T(8,128)(2,1)S(1)} copy-done((bf16[2,512,1024]{2,1,0:T(8,128)(2,1)S(1)}, bf16[2,512,1024]{2,1,0:T(8,128)(2,1)}, u32[]{:S(2)}) %copy-start) | copy-done | bytes 2097176
  2.9 0.0 copy-start.1
  2.9 1.6 %copy-done.1 = bf16[2,1024,512]{2,1,0:T(8,128)(2,1)S(1)} copy-done((bf16[2,1024,512]{2,1,0:T(8,128)(2,1)S(1)}, bf16[2,1024,512]{2,1,0:T(8,128)(2,1)}, u32[]{:S(2)}) %copy-start.1) | copy-done | bytes 2097176
  4.5 0.0 copy-start.2
  4.5 1.2 %copy-done.2 = s32[128,2048]{1,0:T(8,128)S(1)} copy-done((s32[128,2048]{1,0:T(8,128)S(1)}, s32[128,2048]{1,0:T(8,128)}, u32[]{:S(2)}) %copy-start.2) | copy-done | bytes 1048600
  5.7 0.0 copy-start.3
  5.7 0.9 copy-done.3
  6.6 0.0 copy-start.4
  6.6 0.8 copy-done.4
  7.4 0.0 copy-start.5
  7.4 0.7 copy-done.5
  8.1 111.9 %shard_map.122 = (f32[128,128]{1,0:T(8,128)S(1)}, f32[2,128,128]{2,1,0:T(8,128)S(1)}) custom-call(f32[128,128]{1,0:T(8,128)S(1)} %copy-done.4, s32[128,2048]{1,0:T(8,128)S(1)} %copy-done.2, f32[2,32,512]{2,1,0:T(8,128)S(1)} %bitcast.3, f32[1]{0:T(128)S(6)} %copy.14.weight_ref, f32[2]{0:T(128)S(1)} %copy-done.5, bf16[2,1024,512]{2,1,0:T(8,128)(2,1)S(1)} %copy-done.1, ...), custom_call_target="tpu_custom_call" | custom-call | tf_op jit(solution)/shard_map/pallas_call | solution.py:470
  120.0 0.8 add_divide_fusion
  120.8 0.6 copy.15
Async XLA Ops:
  1.3 1.6 %copy-start = (bf16[2,512,1024]{2,1,0:T(8,128)(2,1)S(1)}, bf16[2,512,1024]{2,1,0:T(8,128)(2,1)}, u32[]{:S(2)}) copy-start(bf16[2,512,1024]{2,1,0:T(8,128)(2,1)} %constant.19.clone.rest_1_) | copy-start | bytes 6291460
  2.9 1.6 %copy-start.1 = (bf16[2,1024,512]{2,1,0:T(8,128)(2,1)S(1)}, bf16[2,1024,512]{2,1,0:T(8,128)(2,1)}, u32[]{:S(2)}) copy-start(bf16[2,1024,512]{2,1,0:T(8,128)(2,1)} %constant.18.clone.rest_0_) | copy-start | bytes 6291460
  4.5 1.2 %copy-start.2 = (s32[128,2048]{1,0:T(8,128)S(1)}, s32[128,2048]{1,0:T(8,128)}, u32[]{:S(2)}) copy-start(s32[128,2048]{1,0:T(8,128)} %target_hbm.1) | copy-start | bytes 3145732
  5.7 0.9 copy-start.3
  6.6 0.8 copy-start.4
  7.4 0.7 copy-start.5

commit v3 on v2

--- a/solution.py
+++ b/solution.py
@@ -237,16 +237,20 @@
     def given(phase, buffer):
         pltpu.make_async_copy(buffer, buffer, send_sem.at[phase]).wait()
 
-    def direct(phase, copy, dst, is_own):
-        for dx in (2, 1, 3, 0):
-            for dy in (2, 1, 3, 0):
-                for db, dz in ((1, 1), (1, 0), (0, 1), (0, 0)):
-                    to_kappa = lax.rem(z_lo + dz, 2) * 4 + lax.rem(x_at + dx, 4)
-                    src, where = copy(to_kappa, lax.rem(y_at + dy, 4), db)
-                    if (dx, dy, db, dz) == (0, 0, 0, 0):
-                        maybe_own(phase, src, dst, where, is_own)
-                    else:
-                        send(phase, src, dst, where)
+    steps_apart = (2, 1, 3, 0)
+    nested = [
+        (dx, dy, db, dz) for dx in steps_apart for dy in steps_apart for db, dz in ((1, 1), (1, 0), (0, 1), (0, 0))
+    ]
+    by_distance = sorted(nested, key=lambda d: -(min(d[0], 4 - d[0]) + min(d[1], 4 - d[1]) + 2 * d[2] + d[3]))
+
+    def direct(phase, copy, dst, is_own, order=nested):
+        for dx, dy, db, dz in order:
+            to_kappa = lax.rem(z_lo + dz, 2) * 4 + lax.rem(x_at + dx, 4)
+            src, where = copy(to_kappa, lax.rem(y_at + dy, 4), db)
+            if (dx, dy, db, dz) == (0, 0, 0, 0):
+                maybe_own(phase, src, dst, where, is_own)
+            else:
+                send(phase, src, dst, where)
         sent.append((phase, is_own))
 
     def out_rows(t, carry):
@@ -255,12 +259,22 @@
         return carry
 
     lax.fori_loop(1, KERNS, out_rows, 0, unroll=True)
+
+    own_target = focus == core
+    for q in range(2):
+        maybe_own(
+            1, hs.at[q], hr.at[me_s % 4], device(kappa, core, y_at, core, q), me_s % 4 == 2 * core + q
+        )
+
+    @pl.when(own_target)
+    def _():
+        send(2, ts, tr, device(kappa, core, y_at, 1 - focus, par))
+
     own_block.wait()
     take(0, r0.at[pl.ds(0, KERNS - 1)])
     lo = jnp.concatenate([r0[b] for b in range(8)], 1)
     hi = jnp.concatenate([r0[b] for b in range(8, 16)], 1)
 
-    own_target = focus == core
     for step in range(STEPS):
         base = 5 + 7 * step
         first, last = step == 0, step == STEPS - 1
@@ -278,16 +292,11 @@
             (par == core) & (focus == core),
         )
         if first:
-            for q in range(2):
-                for to_core in range(2):
-                    maybe_own(
-                        1, hs.at[q], hr.at[me_s % 4], device(kappa, to_core, y_at, core, q),
-                        (me_s % 4 == 2 * core + q) & (core == to_core),
-                    )
 
             @pl.when(own_target)
             def _():
-                send(2, ts, tr, device(kappa, core, y_at, 1 - focus, par))
+                take(1, hr)
+                send(19, hr, hr, sibling)
 
             loads[1].wait()
         take(base, r_a.at[step])
@@ -295,7 +304,11 @@
         s_sp[step] = low(part)
         send(base + 1, s_sp.at[step], r_sp.at[step], sibling)
         if first:
-            take(1, hr)
+
+            @pl.when(jnp.logical_not(own_target))
+            def _():
+                take(19, hr)
+
             flat = jnp.concatenate(
                 [hr[z, 16 * c : 16 * c + 16, :] for c in range(2) for z in range(4)], 0
             )
@@ -373,6 +386,12 @@
             return s_db.at[step, to_par * 32 + y * 8 + k], device(k, core, y, focus, to_par)
 
         direct(base + 3, back_out, r_db.at[step, place], True)
+        take(base + 3, r_db.at[step])
+
+        g = to_spectrum(r_db[step].reshape(HALF, 128), t_freq, roll)
+        part = h_re[...] * g - h_im[...] * roll(g)
+        s_d[step] = low(part)
+        send(base + 4, s_d.at[step], r_d.at[step], sibling)
         if last:
             home = 4 * y_at + 2 * core + par
             maybe_own(3, s9.at[me_k], r9.at[focus * 8 + kappa], (me_k, home), own_target)
@@ -383,12 +402,6 @@
                 return carry
 
             lax.fori_loop(1, KERNS, light_home, 0, unroll=True)
-        take(base + 3, r_db.at[step])
-
-        g = to_spectrum(r_db[step].reshape(HALF, 128), t_freq, roll)
-        part = h_re[...] * g - h_im[...] * roll(g)
-        s_d[step] = low(part)
-        send(base + 4, s_d.at[step], r_d.at[step], sibling)
         take(base + 4, r_d.at[step])
         low_rows, high_rows = to_pixel_rows(part + wide(r_d[step]), t_rows, roll)
         s_da[step, :32] = low_rows.reshape(32, 16, 128)
@@ -399,7 +412,8 @@
             return s_da.at[step, at], device(k, par, y, core, to_par)
 
         direct(
-            base + 5, adjoint_out, r_da.at[step, focus * 32 + y_at * 8 + kappa], (par == core) & (focus == core)
+            base + 5, adjoint_out, r_da.at[step, focus * 32 + y_at * 8 + kappa], (par == core) & (focus == core),
+            by_distance,
         )
         if first:
             loads[5].wait()
@@ -434,8 +448,8 @@
 
     given(0, r0.at[pl.ds(0, KERNS - 1)])
     for q in range(2):
-        for to_core in range(2):
-            sent_maybe(1, hs.at[q], (me_s % 4 == 2 * core + q) & (core == to_core))
+        sent_maybe(1, hs.at[q], me_s % 4 == 2 * core + q)
+    sent_maybe(19, hr, jnp.logical_not(own_target))
     sent_maybe(2, ts, jnp.logical_not(own_target))
     given(3, s9.at[pl.ds(0, KERNS - 1)])
     sent_maybe(3, s9.at[0], own_target)
@@ -499,11 +513,11 @@
         + exchange
         + [
             pltpu.SemaphoreType.DMA((9,)),
-            pltpu.SemaphoreType.DMA((19,)),
-            pltpu.SemaphoreType.DMA((19,)),
+            pltpu.SemaphoreType.DMA((20,)),
+            pltpu.SemaphoreType.DMA((20,)),
         ],
         compiler_params=pltpu.CompilerParams(
-            collective_id=0, has_side_effects=True, vmem_limit_bytes=48 * 1024 * 1024
+            collective_id=0, has_side_effects=True, vmem_limit_bytes=62 * 1024 * 1024
         ),
     )(mask_params, target_bits, kernels[0].transpose(0, 2, 1), weights, dose_factors, *consts)
     printed = jax.nn.sigmoid(

time: 122 us -> 117 us (0.959)
  local copies, waits for them, and re-layouts: 7.43 us -> 1.48 us
    unnamed x13 -> x3, local copies, waits for them, and re-layouts: 7.43 us -> 1.48 us
where the time goes in v3:
time: 117 us; the launch traced here: 116 us
  Pallas kernels  112 us (96%)
  other arithmetic  1.75 us (1%)
  local copies, waits for them, and re-layouts  1.48 us (1%)
  between operations  1.3 us (1%)
    pallas_call x1, Pallas kernels, body(): pl.pallas_call(kernel, out_shape=(jax.ShapeDtypeStruct((128, 128), f32),...  112 us

profile of v3, /device:TPU:1, one launch (start us, length us, event | category | flops | bytes accessed | tf_op | source)
XLA Modules:
  0.0 116.4 jit_solution(5446389331340148613)
XLA Ops:
  1.3 0.0 copy-start
  1.3 111.8 %shard_map.122 = (f32[128,128]{1,0:T(8,128)}, f32[2,128,128]{2,1,0:T(8,128)}) custom-call(f32[128,128]{1,0:T(8,128)} %mask_hbm.1, s32[128,2048]{1,0:T(8,128)} %target_hbm.1, f32[2,32,512]{2,1,0:T(8,128)} %bitcast.3, f32[1]{0:T(128)S(6)} %copy.14.weight_ref, f32[2]{0:T(128)} %dose_ref.1, bf16[2,1024,512]{2,1,0:T(8,128)(2,1)} %constant.18.clone.rest_0_, ...), custom_call_target="tpu_custom_call" | custom-call | tf_op jit(solution)/shard_map/pallas_call | solution.py:484
  113.1 0.0 copy-done
  113.1 1.8 %add_divide_fusion = f32[2,2,128,128]{3,2,1,0:T(8,128)} fusion(f32[2,128,128]{2,1,0:T(8,128)} %get-tuple-element.5, f32[2]{0:T(128)S(1)} %copy-done), kind=kLoop, calls=%fused_computation | loop fusion | flops 393216 | bytes 393224 | tf_op jit(solution)/shard_map/div | solution.py:523
  114.9 1.5 %copy.15 = f32[128,128]{1,0:T(8,128)} copy(f32[128,128]{1,0:T(8,128)} %get-tuple-element.8) | data formatting | bytes 131072
Async XLA Ops:
  1.3 111.9 %copy-start = (f32[2]{0:T(128)S(1)}, f32[2]{0:T(128)}, u32[]{:S(2)}) copy-start(f32[2]{0:T(128)} %dose_ref.1) | copy-start | bytes 28

commit v4 on v3

v4 whole, which is shorter than its diff:
```python
import math

import jax
import jax.numpy as jnp
import ml_dtypes
import numpy as np
from jax import lax
from jax.experimental import pallas as pl
from jax.experimental.pallas import tpu as pltpu
from jax.sharding import PartitionSpec as P

N = 2048
F = 512
STEPS = 2
HALF = N // 2
EVEN = F // 2
KERNS = 16
SLABS = 16
PEERS = 64

steepness = 3.0
threshold = 1.0
step_rate = 0.4
MESH = pl.DeviceIdType.MESH


def tables():
    scale = 1.0 / math.sqrt(N)

    def waves(index):
        phases = ((index[:, None] - F // 2) * np.arange(HALF)[None, :]) % N
        angles = phases * (2.0 * math.pi / N)
        return np.cos(angles) * scale, np.sin(angles) * scale

    cos, sin = waves(np.concatenate([np.arange(0, F, 2), np.arange(1, F, 2)]))
    y, z, k, i = np.meshgrid(np.arange(2), np.arange(2), np.arange(8), np.arange(16), indexing="ij")
    rows = [((y * 4 + 2 * h + z) * 128 + k * 16 + i).reshape(-1) for h in range(2)]
    both = np.stack([cos.reshape(2, EVEN, HALF), sin.reshape(2, EVEN, HALF)], 1).reshape(2 * F, HALF)
    to_rows = np.stack([both[:, r].T for r in rows])
    to_freq = to_rows.transpose(0, 2, 1).reshape(2, 2 * F, 32, 2, 8).transpose(0, 1, 3, 2, 4).reshape(2, 2 * F, 512)
    p, y, z, h, t = np.meshgrid(
        np.arange(2), np.arange(4), np.arange(2), np.arange(2), np.arange(16), indexing="ij"
    )
    cos, sin = waves((32 * (4 * y + 2 * h + z) + 2 * t + p).reshape(-1))
    to_cols = np.concatenate([cos, sin], 1)
    from_cols = np.concatenate([cos[:EVEN].T, sin[:EVEN].T, cos[EVEN:].T, sin[EVEN:].T], 1)
    c, s = cos.reshape(2, 8, 32, HALF), sin.reshape(2, 8, 32, HALF)
    mixed = np.stack([c, -s], 2).reshape(2, F, HALF)
    cast = lambda table: np.ascontiguousarray(table).astype(np.float32).astype(ml_dtypes.bfloat16)
    return [cast(t) for t in (mixed.transpose(0, 2, 1), to_freq, to_rows, to_cols, from_cols, mixed)]


def dot(left, right):
    return jnp.dot(left, right, preferred_element_type=jnp.float32)


def low(value):
    return value.astype(jnp.bfloat16)


def wide(value):
    return value.astype(jnp.float32)


def lane(value):
    return lax.broadcasted_iota(jnp.int32, value.shape, len(value.shape) - 1)


def is_front(value):
    return lane(value) < 64


def is_real(value):
    return lane(value) % 64 < 32


def roll(value, by):
    return pltpu.roll(value, by, 1)


def swap(value):
    return jnp.where(is_real(value), roll(value, 96), roll(value, 32))


def fronts(first, second):
    front = is_front(first)
    return jnp.where(front, first, roll(second, 64)), jnp.where(front, roll(first, 64), second)


def columns_spectrum(got, table):
    lo, hi = wide(got[:32].reshape(256, 128)), wide(got[32:].reshape(256, 128))
    parts = []
    for par, x in enumerate((lo + hi, lo - hi)):
        turned = jnp.where(is_real(x), swap(x), -swap(x))
        front = is_front(x)
        both = jnp.concatenate(
            [jnp.where(front, x, roll(turned, 64)), jnp.where(front, roll(x, 64), turned)], 0
        )
        out = dot(table[par * F : par * F + F, :], low(both))
        one = jnp.where(is_front(out[:EVEN]), out[:EVEN], out[EVEN:])
        parts.append(one + roll(one, 64))
    return jnp.concatenate(parts, 0)


def rows_spectrum(got, table):
    lo, hi = wide(got[:32]), wide(got[32:])
    parts = []
    for par, x in enumerate((lo + hi, lo - hi)):
        x = jnp.concatenate([x[:, :8].reshape(256, 128), x[:, 8:].reshape(256, 128)], 0)
        turned = jnp.where(is_real(x), swap(x), -swap(x))
        at = par * F
        parts.append(dot(table[at : at + EVEN, :], low(x)) + dot(table[at + EVEN : at + F, :], low(turned)))
    return jnp.concatenate(parts, 0)


def pixel_rows(spec, table):
    turned = jnp.where(is_real(spec), -swap(spec), swap(spec))
    parts = []
    for par in range(2):
        rows = slice(par * EVEN, par * EVEN + EVEN)
        both = low(jnp.concatenate([spec[rows], turned[rows]], 0))
        parts.append(dot(table[:, par * F : par * F + F], both))
    return parts[0] + parts[1], parts[0] - parts[1]


def side_by_side(rows):
    rows = rows.reshape(32, 2, 8, 128)
    return low(jnp.where(is_front(rows[:, 0]), rows[:, 0], rows[:, 1]))


def regroup(tiles):
    a, c = fronts(tiles[0], tiles[2])
    b, d = fronts(tiles[1], tiles[3])
    out = []
    for p, q in ((a, b), (c, d)):
        real = is_real(p)
        out += [jnp.where(real, p, roll(q, 32)), jnp.where(real, roll(p, 96), q)]
    return out


def field(lefts, table, chunk):
    fields = []
    for par, left in enumerate(lefts):
        rows = slice(par * EVEN, par * EVEN + EVEN)
        with_cos = dot(left, table[rows, chunk * 256 : chunk * 256 + 256])
        with_sin = dot(left, table[rows, HALF + chunk * 256 : HALF + chunk * 256 + 256])
        fields.append((with_cos[:128] - with_sin[128:], with_cos[128:] + with_sin[:128]))
    (e_re, e_im), (o_re, o_im) = fields
    return (e_re + o_re, e_im + o_im), (e_re - o_re, e_im - o_im)


def light(e):
    power = e[0] * e[0] + e[1] * e[1]
    return jnp.sum(power.reshape(8, 16, 256), axis=0)


def sensitivity(intensity, target, doses):
    total = 0.0
    for dose in doses:
        printed = jax.nn.sigmoid(steepness * (dose * intensity - threshold))
        total = total + (printed - target) * printed * (1.0 - printed) * (steepness * dose)
    return total


def cotangent(e, sens):
    spread = jnp.broadcast_to((2.0 * sens)[None], (8, 16, 256)).reshape(128, 256)
    return jnp.concatenate([spread * e[0], spread * e[1]], 0)


def back_columns(lo, hi, table, chunk):
    rows = slice(chunk * 256, chunk * 256 + 256)
    return dot(low(lo + hi), table[rows, :F]), dot(low(lo - hi), table[rows, F:])


def back_parts(part):
    return part[:128, :EVEN] + part[128:, EVEN:], part[128:, :EVEN] - part[:128, EVEN:]


def grad_part(got, table):
    blocks = jnp.sum(wide(got).reshape(8, 8, 8, 128), axis=1)
    tiles = [jnp.concatenate(fronts(blocks[2 * j], blocks[2 * j + 1]), 0) for j in range(4)]
    return dot(low(jnp.concatenate(tiles, 1)), table[:, :])


def kernel(mask_hbm, target_hbm, h_hbm, weight_ref, dose_ref, *rest):
    table_hbm = rest[:6]
    params_out, light_out = rest[6:8]
    (
        t_mask, t_freq_a, t_freq_b, t_rows_a, t_rows_b, t_cols, t_back, t_mix,
        h_raw, h_re, h_im, h_turn, target, acc,
        r0, hs, hr, s9, r9, s10, r10,
        s_a, r_a, s_sp, r_sp, s_b, r_b, s_db, r_db, s_d, r_d, s_da, r_da, s_g, r_g,
        local_sem, send_sem, recv_sem,
    ) = rest[8:]
    me_k, me_s = lax.axis_index("kern"), lax.axis_index("slab")
    kappa, core = me_k // 2, me_k % 2
    z0, x_at = kappa // 4, kappa % 4
    y_at, z2, z1 = me_s // 4, (me_s % 4) // 2, me_s % 2
    place = y_at * 16 + z1 * 8 + kappa
    block = 2 * y_at + z1
    sign = (1 - 2 * core).astype(jnp.float32)

    def device(x, y, z2, z1, z0, core):
        return (2 * (4 * z0 + x) + core, 4 * y + 2 * z2 + z1)

    sibling = (me_k + 1 - 2 * core, me_s)

    barrier = pltpu.get_barrier_semaphore()

    def greet(t, carry):
        slab = lax.rem(me_s + t, SLABS)
        kern = lax.rem(me_k + t, KERNS)
        pl.semaphore_signal(barrier, inc=1, device_id=(me_k, slab), device_id_type=MESH)
        pl.semaphore_signal(barrier, inc=1, device_id=(kern, me_s), device_id_type=MESH)
        return carry

    pl.semaphore_signal(
        barrier, inc=1, device_id=device(x_at, y_at, 1 - z2, z1, 1 - z0, core), device_id_type=MESH
    )
    lax.fori_loop(1, 16, greet, 0)

    own_block = pltpu.make_async_copy(
        mask_hbm.at[pl.ds(pl.multiple_of(16 * kappa, 16), 16)], r0.at[me_k], local_sem.at[8]
    )
    load_target = pltpu.make_async_copy(
        target_hbm.at[pl.ds(pl.multiple_of(16 * kappa, 16), 16)], target, local_sem.at[9]
    )
    loads = [
        pltpu.make_async_copy(src, dst, local_sem.at[n])
        for n, (src, dst) in enumerate(
            (
                (table_hbm[0].at[core], t_mask),
                (table_hbm[1].at[core], t_freq_a),
                (table_hbm[2].at[z2], t_rows_b),
                (table_hbm[3], t_cols),
                (table_hbm[4], t_back),
                (table_hbm[1].at[z2], t_freq_b),
                (table_hbm[2].at[core], t_rows_a),
                (table_hbm[5].at[core], t_mix),
            )
        )
    ]
    own_block.start()
    for b in range(4):
        pltpu.make_async_copy(h_hbm.at[:, :, pl.ds(128 * b, 128)], h_raw.at[b], local_sem.at[10]).start()
    for load in loads:
        load.start()
    load_target.start()

    pltpu.make_async_copy(h_raw, h_raw, local_sem.at[10]).wait()
    root = jnp.sqrt(jnp.full((16, 128), weight_ref[0], jnp.float32))
    for q in range(2):
        for part in range(2):
            for b in range(4):
                own_rows = h_raw[b, part, pl.ds(q, 16, stride=2), :]
                hs[q, 16 * part : 16 * part + 16, 128 * b : 128 * b + 128] = low(own_rows * root)

    pl.semaphore_wait(barrier, 31)

    sent = []

    def send(phase, src, dst, where):
        pltpu.make_async_remote_copy(
            src_ref=src, dst_ref=dst, send_sem=send_sem.at[phase], recv_sem=recv_sem.at[phase],
            device_id=where, device_id_type=MESH,
        ).start()

    def maybe_own(phase, src, dst, where, is_own):
        if is_own is True:
            pltpu.make_async_copy(src, dst, recv_sem.at[phase]).start()
            return

        @pl.when(is_own)
        def _():
            pltpu.make_async_copy(src, dst, recv_sem.at[phase]).start()

        @pl.when(jnp.logical_not(is_own))
        def _():
            send(phase, src, dst, where)

    def sent_maybe(phase, buffer, is_own):
        @pl.when(jnp.logical_not(is_own))
        def _():
            pltpu.make_async_copy(buffer, buffer, send_sem.at[phase]).wait()

    def take(phase, buffer):
        pltpu.make_async_copy(buffer, buffer, recv_sem.at[phase]).wait()

    def given(phase, buffer):
        pltpu.make_async_copy(buffer, buffer, send_sem.at[phase]).wait()

    steps_apart = (2, 1, 3, 0)
    nested = [
        (dx, dy, da, db) for dx in steps_apart for dy in steps_apart for da, db in ((1, 1), (1, 0), (0, 1), (0, 0))
    ]

    def direct(phase, copy, dst, is_own):
        for dx, dy, da, db in nested:
            src, where = copy(lax.rem(x_at + dx, 4), lax.rem(y_at + dy, 4), da, db)
            if (dx, dy, da, db) == (0, 0, 0, 0):
                maybe_own(phase, src, dst, where, is_own)
            else:
                send(phase, src, dst, where)
        sent.append((phase, is_own))

    def flip(bit, by):
        return 1 - bit if by else bit

    def out_rows(t, carry):
        kern = lax.rem(me_k + t, KERNS)
        send(0, mask_hbm.at[pl.ds(pl.multiple_of(16 * (kern // 2), 16), 16)], r0.at[me_k], (kern, me_s))
        return carry

    lax.fori_loop(1, KERNS, out_rows, 0, unroll=True)

    for dq, dz in ((1, 1), (0, 1), (1, 0), (0, 0)):
        to_par = flip(z0, dq)
        where = device(x_at, y_at, flip(z2, dz), z1, to_par, core)
        if dq or dz:
            send(1, hs.at[to_par], hr.at[2 * z0 + z2], where)
        else:
            maybe_own(1, hs.at[to_par], hr.at[2 * z0 + z2], where, True)

    own_block.wait()
    take(0, r0.at[pl.ds(0, KERNS - 1)])
    lo = jnp.concatenate([r0[b] for b in range(8)], 1)
    hi = jnp.concatenate([r0[b] for b in range(8, 16)], 1)

    owner_is_reader = (z0 == core) & (z2 == core)
    for step in range(STEPS):
        base = 5 + 7 * step
        first, last = step == 0, step == STEPS - 1

        mask_lo, mask_hi = jnp.tanh(lo), jnp.tanh(hi)
        if first:
            loads[0].wait()
        columns = dot(low(mask_lo + sign * mask_hi), t_mask[...])
        for j in range(4):
            tile = columns[:, 128 * j : 128 * j + 128]
            front, back = fronts(tile[:8], tile[8:])
            s_a[step, 2 * j] = low(front)
            s_a[step, 2 * j + 1] = low(back)

        def columns_out(x, y, da, db):
            to_z1 = flip(z1, db)
            return s_a.at[step, 2 * y + to_z1], device(x, y, flip(z2, da), to_z1, core, z2)

        direct(base, columns_out, r_a.at[step, place], owner_is_reader)
        if first:
            loads[1].wait()
        take(base, r_a.at[step])
        part = columns_spectrum(r_a[step], t_freq_a)
        s_sp[step] = low(part)
        send(base + 1, s_sp.at[step], r_sp.at[step], sibling)
        if first:
            take(1, hr)
            flat = jnp.concatenate(
                [hr[2 * k + h, 16 * c : 16 * c + 16, :] for k in range(2) for c in range(2) for h in range(2)], 0
            )
            h_turn[...] = wide(flat).T
            for q in range(2):
                rows = slice(q * EVEN, q * EVEN + EVEN)
                h = h_turn[pl.ds(q, EVEN, stride=2), :]
                swapped = swap(h)
                h_re[rows, :] = jnp.where(is_real(h), h, swapped)
                h_im[rows, :] = jnp.where(is_real(h), -swapped, h)
            loads[2].wait()
        take(base + 1, r_sp.at[step])
        spec = part + wide(r_sp[step])

        filtered = h_re[...] * spec + h_im[...] * swap(spec)
        low_rows, high_rows = pixel_rows(filtered, t_rows_b)
        s_b[step, :32] = low(low_rows).reshape(32, 16, 128)
        s_b[step, 32:] = low(high_rows).reshape(32, 16, 128)

        def rows_out(x, y, da, db):
            to_z1, to_z0 = flip(z1, da), flip(z0, db)
            return s_b.at[step, y * 16 + to_z1 * 8 + to_z0 * 4 + x], device(x, y, z2, to_z1, to_z0, core)

        direct(base + 2, rows_out, r_b.at[step, z0 * 32 + block * 4 + x_at], True)
        if first:
            loads[3].wait()
            loads[4].wait()
            load_target.wait()
        take(base + 2, r_b.at[step])

        lefts = []
        for q in range(2):
            groups = []
            for m in range(2):
                tiles = [32 * q + 16 * m + 4 * g for g in range(4)]
                groups.append(regroup([wide(r_b[step, at : at + 4]).reshape(64, 128) for at in tiles]))
            order = [jnp.concatenate([groups[0][n], groups[1][n]], 1) for n in (0, 2, 1, 3)]
            lefts.append(low(jnp.concatenate(order, 0)))
        doses = [dose_ref[d] for d in range(2)]
        for chunk in range(4):
            cots = []
            for n, e in enumerate(field(lefts, t_cols, chunk)):
                intensity = light(e)
                start = n * HALF + 256 * chunk
                if last:
                    for m in range(2):
                        s9[start // 128 + m] = low(intensity[:, 128 * m : 128 * m + 128])
                sens = sensitivity(intensity, wide(target[:, start : start + 256]), doses)
                cots.append(cotangent(e, sens))
            for q, term in enumerate(back_columns(cots[0], cots[1], t_back, chunk)):
                if chunk == 0:
                    acc[q] = term
                else:
                    acc[q] += term
        for q in range(2):
            re, im = back_parts(acc[q])
            for m in range(2):
                lanes = slice(128 * m, 128 * m + 128)
                tiles = regroup([re[:64, lanes], im[:64, lanes], re[64:, lanes], im[64:, lanes]])
                for g, tile in enumerate(tiles):
                    at = 32 * q + 16 * m + 4 * g
                    s_db[step, at : at + 4] = low(tile).reshape(4, 16, 128)

        def back_out(x, y, da, db):
            to_z1, to_z0 = flip(z1, da), flip(z0, db)
            return s_db.at[step, to_z0 * 32 + (2 * y + to_z1) * 4 + x], device(x, y, z2, to_z1, to_z0, core)

        direct(base + 3, back_out, r_db.at[step, place], True)
        if first:
            loads[5].wait()
        take(base + 3, r_db.at[step])

        g = rows_spectrum(r_db[step], t_freq_b)
        part = h_re[...] * g - h_im[...] * swap(g)
        part = part + roll(part, 64)
        s_d[step] = low(part)
        send(base + 4, s_d.at[step], r_d.at[step], sibling)
        if first:
            loads[6].wait()
        if last:
            maybe_own(3, s9.at[me_k], r9.at[core * 8 + kappa], (me_k, me_s), True)

            def light_home(t, carry):
                kern = lax.rem(me_k + t, KERNS)
                send(3, s9.at[kern], r9.at[core * 8 + kappa], (kern, me_s))
                return carry

            lax.fori_loop(1, KERNS, light_home, 0, unroll=True)
        take(base + 4, r_d.at[step])
        low_rows, high_rows = pixel_rows(part + wide(r_d[step]), t_rows_a)
        s_da[step, :32] = side_by_side(low_rows)
        s_da[step, 32:] = side_by_side(high_rows)

        def adjoint_out(x, y, da, db):
            to_z1, to_z0 = flip(z1, da), flip(z0, db)
            return s_da.at[step, y * 16 + to_z1 * 8 + to_z0 * 4 + x], device(x, y, core, to_z1, to_z0, z0)

        direct(base + 5, adjoint_out, r_da.at[step, block * 8 + z2 * 4 + x_at], owner_is_reader)
        if first:
            loads[7].wait()
        take(base + 5, r_da.at[step])

        own = grad_part(r_da[step], t_mix)
        s_g[step] = own
        send(base + 6, s_g.at[step], r_g.at[step], sibling)
        take(base + 6, r_g.at[step])
        other = r_g[step]
        lo = lo - step_rate * (own + other) * (1.0 - mask_lo * mask_lo)
        hi = hi - step_rate * (sign * (own - other)) * (1.0 - mask_hi * mask_hi)

    for b in range(8):
        s10[b] = lo[:, 128 * b : 128 * b + 128]
        s10[b + 8] = hi[:, 128 * b : 128 * b + 128]
    at_home = me_k // 8 == core
    kern = 8 * core + me_k % 8
    maybe_own(4, s10.at[kern], r10.at[kappa], (kern, me_s), at_home)

    def params_home(t, carry):
        kern = 8 * core + lax.rem(me_k + t, 8)
        send(4, s10.at[kern], r10.at[kappa], (kern, me_s))
        return carry

    lax.fori_loop(1, 8, params_home, 0, unroll=True)
    take(3, r9)
    for k in range(KERNS):
        light_out[k // 8, 16 * (k % 8) : 16 * (k % 8) + 16, :] = wide(r9[k])
    take(4, r10)
    params_out[...] = r10[...].reshape(128, 128)

    given(0, r0.at[pl.ds(0, KERNS - 1)])
    given(1, hr.at[pl.ds(0, 3)])
    given(3, s9.at[pl.ds(0, KERNS - 1)])
    given(4, s10.at[pl.ds(0, 7)])
    sent_maybe(4, s10.at[0], at_home)
    for phase, is_own in sent:
        if is_own is True:
            given(phase, r_b.at[0, pl.ds(0, PEERS - 1)])
        else:
            given(phase, r_a.at[0, pl.ds(0, PEERS - 1)])
            sent_maybe(phase, r_a.at[0, 0], is_own)
    for step in range(STEPS):
        given(5 + 7 * step + 1, s_sp.at[step])
        given(5 + 7 * step + 4, s_d.at[step])
        given(5 + 7 * step + 6, s_g.at[step])


def body(mask_params, target_bits, kernels, weights, dose_factors):
    f32, bf16 = jnp.float32, jnp.bfloat16
    consts = [jnp.asarray(t) for t in tables()]
    hbm, vmem = pl.BlockSpec(memory_space=pl.ANY), pl.BlockSpec(memory_space=pltpu.VMEM)
    smem = pl.BlockSpec(memory_space=pltpu.SMEM)
    exchange = []
    for shape, send_shape, kind in (
        ((PEERS, 8, 128), (8, 8, 128), bf16),
        ((F, 128), (F, 128), bf16),
        ((PEERS, 16, 128), (PEERS, 16, 128), bf16),
        ((PEERS, 16, 128), (PEERS, 16, 128), bf16),
        ((F, 128), (F, 128), bf16),
        ((PEERS, 8, 128), (PEERS, 8, 128), bf16),
        ((16, HALF), (16, HALF), f32),
    ):
        exchange += [pltpu.VMEM((STEPS,) + send_shape, kind), pltpu.VMEM((STEPS,) + shape, kind)]
    params, intensity = pl.pallas_call(
        kernel,
        out_shape=(jax.ShapeDtypeStruct((128, 128), f32), jax.ShapeDtypeStruct((2, 128, 128), f32)),
        in_specs=[hbm, hbm, hbm, smem, smem] + [hbm] * 6,
        out_specs=(vmem, vmem),
        scratch_shapes=[
            pltpu.VMEM((HALF, F), bf16),
            pltpu.VMEM((HALF, F), bf16),
            pltpu.VMEM((HALF, F), bf16),
            pltpu.VMEM((F, HALF), bf16),
            pltpu.VMEM((F, HALF), bf16),
            pltpu.VMEM((F, N), bf16),
            pltpu.VMEM((HALF, HALF), bf16),
            pltpu.VMEM((F, HALF), bf16),
            pltpu.VMEM((4, 2, 32, 128), f32),
            pltpu.VMEM((F, 128), f32),
            pltpu.VMEM((F, 128), f32),
            pltpu.VMEM((F, 128), f32),
            pltpu.VMEM((16, N), jnp.int32),
            pltpu.VMEM((2, 256, F), f32),
            pltpu.VMEM((16, 16, 128), f32),
            pltpu.VMEM((2, 32, F), bf16),
            pltpu.VMEM((4, 32, F), bf16),
            pltpu.VMEM((16, 16, 128), bf16),
            pltpu.VMEM((16, 16, 128), bf16),
            pltpu.VMEM((16, 16, 128), f32),
            pltpu.VMEM((8, 16, 128), f32),
        ]
        + exchange
        + [
            pltpu.SemaphoreType.DMA((11,)),
            pltpu.SemaphoreType.DMA((19,)),
            pltpu.SemaphoreType.DMA((19,)),
        ],
        compiler_params=pltpu.CompilerParams(
            collective_id=0, has_side_effects=True, vmem_limit_bytes=62 * 1024 * 1024
        ),
    )(mask_params, target_bits, kernels[0].transpose(0, 2, 1), weights, dose_factors, *consts)
    printed = jax.nn.sigmoid(
        steepness * (dose_factors[None, :, None, None] * intensity[:, None] - threshold)
    )
    return params, printed


def solution(mesh):
    in_specs = (P("slab", "kern"), P("slab", None), P("kern", None, None, "slab"), P("kern"), P())
    out_specs = (P("slab", "kern"), P(None, None, "slab", "kern"))
    return jax.shard_map(body, mesh=mesh, in_specs=in_specs, out_specs=out_specs, check_vma=False)
```

time: 117 us -> 109 us (0.932)
  Pallas kernels: 112 us -> 104 us
    pallas_call x1, Pallas kernels: 112 us -> 104 us  [body(): pl.pallas_call(kernel, out_shape=(jax.ShapeDtypeStruct((128, 128), f32),...]
where the time goes in v4:
time: 109 us
  Pallas kernels  104 us (95%)
  other arithmetic  1.75 us (2%)
  local copies, waits for them, and re-layouts  1.48 us (1%)
  between operations  1.3 us (1%)
    pallas_call x1, Pallas kernels, body(): pl.pallas_call(kernel, out_shape=(jax.ShapeDtypeStruct((128, 128), f32),...  104 us

profile of v4, /device:TPU:1, one launch (start us, length us, event | category | flops | bytes accessed | tf_op | source)
XLA Modules:
  0.0 108.7 jit_solution(3183145944697831955)
XLA Ops:
  1.3 0.0 copy-start
  1.3 104.1 %shard_map.122 = (f32[128,128]{1,0:T(8,128)}, f32[2,128,128]{2,1,0:T(8,128)}) custom-call(f32[128,128]{1,0:T(8,128)} %mask_hbm.1, s32[128,2048]{1,0:T(8,128)} %target_hbm.1, f32[2,32,512]{2,1,0:T(8,128)} %bitcast.3, f32[1]{0:T(128)S(6)} %copy.14.weight_ref, f32[2]{0:T(128)} %dose_ref.1, bf16[2,1024,512]{2,1,0:T(8,128)(2,1)} %constant.18.clone.rest_0_, ...), custom_call_target="tpu_custom_call" | custom-call | tf_op jit(solution)/shard_map/pallas_call | solution.py:519
  105.4 0.0 copy-done
  105.5 1.8 %add_divide_fusion = f32[2,2,128,128]{3,2,1,0:T(8,128)} fusion(f32[2,128,128]{2,1,0:T(8,128)} %get-tuple-element.5, f32[2]{0:T(128)S(1)} %copy-done), kind=kLoop, calls=%fused_computation | loop fusion | flops 393216 | bytes 393224 | tf_op jit(solution)/shard_map/div | solution.py:557
  107.2 1.5 %copy.15 = f32[128,128]{1,0:T(8,128)} copy(f32[128,128]{1,0:T(8,128)} %get-tuple-element.8) | data formatting | bytes 131072
Async XLA Ops:
  1.3 104.2 %copy-start = (f32[2]{0:T(128)S(1)}, f32[2]{0:T(128)}, u32[]{:S(2)}) copy-start(f32[2]{0:T(128)} %dose_ref.1) | copy-start | bytes 28

commit v5 on v4

--- a/solution.py
+++ b/solution.py
@@ -87,40 +87,25 @@
     return jnp.where(front, first, roll(second, 64)), jnp.where(front, roll(first, 64), second)
 
 
-def columns_spectrum(got, table):
-    lo, hi = wide(got[:32].reshape(256, 128)), wide(got[32:].reshape(256, 128))
-    parts = []
-    for par, x in enumerate((lo + hi, lo - hi)):
-        turned = jnp.where(is_real(x), swap(x), -swap(x))
-        front = is_front(x)
-        both = jnp.concatenate(
-            [jnp.where(front, x, roll(turned, 64)), jnp.where(front, roll(x, 64), turned)], 0
-        )
-        out = dot(table[par * F : par * F + F, :], low(both))
-        one = jnp.where(is_front(out[:EVEN]), out[:EVEN], out[EVEN:])
-        parts.append(one + roll(one, 64))
-    return jnp.concatenate(parts, 0)
-
-
-def rows_spectrum(got, table):
-    lo, hi = wide(got[:32]), wide(got[32:])
-    parts = []
-    for par, x in enumerate((lo + hi, lo - hi)):
-        x = jnp.concatenate([x[:, :8].reshape(256, 128), x[:, 8:].reshape(256, 128)], 0)
-        turned = jnp.where(is_real(x), swap(x), -swap(x))
-        at = par * F
-        parts.append(dot(table[at : at + EVEN, :], low(x)) + dot(table[at + EVEN : at + F, :], low(turned)))
-    return jnp.concatenate(parts, 0)
-
-
-def pixel_rows(spec, table):
+def columns_spectrum(x, table, par):
+    turned = jnp.where(is_real(x), swap(x), -swap(x))
+    front = is_front(x)
+    both = jnp.concatenate([jnp.where(front, x, roll(turned, 64)), jnp.where(front, roll(x, 64), turned)], 0)
+    out = dot(table[par * F : par * F + F, :], low(both))
+    one = jnp.where(is_front(out[:EVEN]), out[:EVEN], out[EVEN:])
+    return one + roll(one, 64)
+
+
+def rows_spectrum(x, table, par):
+    x = jnp.concatenate([x[:, :8].reshape(256, 128), x[:, 8:].reshape(256, 128)], 0)
+    turned = jnp.where(is_real(x), swap(x), -swap(x))
+    at = par * F
+    return dot(table[at : at + EVEN, :], low(x)) + dot(table[at + EVEN : at + F, :], low(turned))
+
+
+def pixel_rows(spec, table, par):
     turned = jnp.where(is_real(spec), -swap(spec), swap(spec))
-    parts = []
-    for par in range(2):
-        rows = slice(par * EVEN, par * EVEN + EVEN)
-        both = low(jnp.concatenate([spec[rows], turned[rows]], 0))
-        parts.append(dot(table[:, par * F : par * F + F], both))
-    return parts[0] + parts[1], parts[0] - parts[1]
+    return dot(table[:, par * F : par * F + F], low(jnp.concatenate([spec, turned], 0)))
 
 
 def side_by_side(rows):
@@ -167,11 +152,6 @@
     return jnp.concatenate([spread * e[0], spread * e[1]], 0)
 
 
-def back_columns(lo, hi, table, chunk):
-    rows = slice(chunk * 256, chunk * 256 + 256)
-    return dot(low(lo + hi), table[rows, :F]), dot(low(lo - hi), table[rows, F:])
-
-
 def back_parts(part):
     return part[:128, :EVEN] + part[128:, EVEN:], part[128:, :EVEN] - part[:128, EVEN:]
 
@@ -184,14 +164,14 @@
 
 def kernel(mask_hbm, target_hbm, h_hbm, weight_ref, dose_ref, *rest):
     table_hbm = rest[:6]
-    params_out, light_out = rest[6:8]
+    params_out, grad_out, light_out = rest[6:9]
     (
         t_mask, t_freq_a, t_freq_b, t_rows_a, t_rows_b, t_cols, t_back, t_mix,
-        h_raw, h_re, h_im, h_turn, target, acc,
-        r0, hs, hr, s9, r9, s10, r10,
+        h_raw, h_re, h_im, h_turn, target, cots,
+        home, s0, r0, r_par, hs, hr, s9, r9, s10, r10, s11, r11,
         s_a, r_a, s_sp, r_sp, s_b, r_b, s_db, r_db, s_d, r_d, s_da, r_da, s_g, r_g,
         local_sem, send_sem, recv_sem,
-    ) = rest[8:]
+    ) = rest[9:]
     me_k, me_s = lax.axis_index("kern"), lax.axis_index("slab")
     kappa, core = me_k // 2, me_k % 2
     z0, x_at = kappa // 4, kappa % 4
@@ -219,9 +199,7 @@
     )
     lax.fori_loop(1, 16, greet, 0)
 
-    own_block = pltpu.make_async_copy(
-        mask_hbm.at[pl.ds(pl.multiple_of(16 * kappa, 16), 16)], r0.at[me_k], local_sem.at[8]
-    )
+    own_block = pltpu.make_async_copy(mask_hbm, home, local_sem.at[8])
     load_target = pltpu.make_async_copy(
         target_hbm.at[pl.ds(pl.multiple_of(16 * kappa, 16), 16)], target, local_sem.at[9]
     )
@@ -247,6 +225,9 @@
         load.start()
     load_target.start()
 
+    own_block.wait()
+    s0[...] = low(jnp.tanh(home[...])).reshape(8, 16, 128)
+
     pltpu.make_async_copy(h_raw, h_raw, local_sem.at[10]).wait()
     root = jnp.sqrt(jnp.full((16, 128), weight_ref[0], jnp.float32))
     for q in range(2):
@@ -303,15 +284,25 @@
                 send(phase, src, dst, where)
         sent.append((phase, is_own))
 
+    def exchange(phase, src, dst, step, q):
+        rows = pl.ds(q * EVEN, EVEN)
+        send(phase, src.at[step, rows], dst.at[step, rows], sibling)
+
     def flip(bit, by):
         return 1 - bit if by else bit
 
     def out_rows(t, carry):
         kern = lax.rem(me_k + t, KERNS)
-        send(0, mask_hbm.at[pl.ds(pl.multiple_of(16 * (kern // 2), 16), 16)], r0.at[me_k], (kern, me_s))
+        send(0, s0.at[kern // 2], r0.at[me_k], (kern, me_s))
         return carry
 
+    def out_params(t, carry):
+        kern = lax.rem(me_k + t, KERNS)
+        send(2, home.at[pl.ds(pl.multiple_of(16 * (kern // 2), 16), 16)], r_par.at[me_k], (kern, me_s))
+        return carry
+
     lax.fori_loop(1, KERNS, out_rows, 0, unroll=True)
+    r0[me_k] = s0[kappa]
 
     for dq, dz in ((1, 1), (0, 1), (1, 0), (0, 0)):
         to_par = flip(z0, dq)
@@ -321,17 +312,18 @@
         else:
             maybe_own(1, hs.at[to_par], hr.at[2 * z0 + z2], where, True)
 
-    own_block.wait()
+    lax.fori_loop(1, KERNS, out_params, 0, unroll=True)
+    r_par[me_k] = home[pl.ds(pl.multiple_of(16 * kappa, 16), 16), :]
     take(0, r0.at[pl.ds(0, KERNS - 1)])
-    lo = jnp.concatenate([r0[b] for b in range(8)], 1)
-    hi = jnp.concatenate([r0[b] for b in range(8, 16)], 1)
-
+    mask_lo = wide(jnp.concatenate([r0[b] for b in range(8)], 1))
+    mask_hi = wide(jnp.concatenate([r0[b] for b in range(8, 16)], 1))
+
+    at_home = me_k // 8 == core
     owner_is_reader = (z0 == core) & (z2 == core)
     for step in range(STEPS):
-        base = 5 + 7 * step
+        base = 5 + 9 * step
         first, last = step == 0, step == STEPS - 1
 
-        mask_lo, mask_hi = jnp.tanh(lo), jnp.tanh(hi)
         if first:
             loads[0].wait()
         columns = dot(low(mask_lo + sign * mask_hi), t_mask[...])
@@ -346,11 +338,32 @@
             return s_a.at[step, 2 * y + to_z1], device(x, y, flip(z2, da), to_z1, core, z2)
 
         direct(base, columns_out, r_a.at[step, place], owner_is_reader)
+        if last:
+            for b in range(8):
+                s10[b] = lo[:, 128 * b : 128 * b + 128]
+                s10[b + 8] = hi[:, 128 * b : 128 * b + 128]
+            kern = 8 * core + me_k % 8
+            maybe_own(5 + 9 * STEPS, s10.at[kern], r10.at[0, kappa], (kern, me_s), at_home)
+
+            def params_home(t, carry):
+                kern = 8 * core + lax.rem(me_k + t, 8)
+                send(5 + 9 * STEPS, s10.at[kern], r10.at[0, kappa], (kern, me_s))
+                return carry
+
+            lax.fori_loop(1, 8, params_home, 0, unroll=True)
         if first:
             loads[1].wait()
+            take(2, r_par.at[pl.ds(0, KERNS - 1)])
+            lo = jnp.concatenate([r_par[b] for b in range(8)], 1)
+            hi = jnp.concatenate([r_par[b] for b in range(8, 16)], 1)
+            mask_lo, mask_hi = jnp.tanh(lo), jnp.tanh(hi)
         take(base, r_a.at[step])
-        part = columns_spectrum(r_a[step], t_freq_a)
-        s_sp[step] = low(part)
+        early, late = wide(r_a[step, :32].reshape(256, 128)), wide(r_a[step, 32:].reshape(256, 128))
+        parts = []
+        for q, x in enumerate((early + late, early - late)):
+            rows = slice(q * EVEN, q * EVEN + EVEN)
+            parts.append(columns_spectrum(x, t_freq_a, q))
+            s_sp[step, rows, :] = low(parts[q])
         send(base + 1, s_sp.at[step], r_sp.at[step], sibling)
         if first:
             take(1, hr)
@@ -365,13 +378,16 @@
                 h_re[rows, :] = jnp.where(is_real(h), h, swapped)
                 h_im[rows, :] = jnp.where(is_real(h), -swapped, h)
             loads[2].wait()
-        take(base + 1, r_sp.at[step])
-        spec = part + wide(r_sp[step])
-
-        filtered = h_re[...] * spec + h_im[...] * swap(spec)
-        low_rows, high_rows = pixel_rows(filtered, t_rows_b)
-        s_b[step, :32] = low(low_rows).reshape(32, 16, 128)
-        s_b[step, 32:] = low(high_rows).reshape(32, 16, 128)
+
+        halves = []
+        for q in range(2):
+            rows = slice(q * EVEN, q * EVEN + EVEN)
+            if q == 0:
+                take(base + 1, r_sp.at[step])
+            spec = parts[q] + wide(r_sp[step, rows, :])
+            halves.append(pixel_rows(h_re[rows, :] * spec + h_im[rows, :] * swap(spec), t_rows_b, q))
+        s_b[step, :32] = low(halves[0] + halves[1]).reshape(32, 16, 128)
+        s_b[step, 32:] = low(halves[0] - halves[1]).reshape(32, 16, 128)
 
         def rows_out(x, y, da, db):
             to_z1, to_z0 = flip(z1, da), flip(z0, db)
@@ -394,7 +410,7 @@
             lefts.append(low(jnp.concatenate(order, 0)))
         doses = [dose_ref[d] for d in range(2)]
         for chunk in range(4):
-            cots = []
+            both = []
             for n, e in enumerate(field(lefts, t_cols, chunk)):
                 intensity = light(e)
                 start = n * HALF + 256 * chunk
@@ -402,14 +418,11 @@
                     for m in range(2):
                         s9[start // 128 + m] = low(intensity[:, 128 * m : 128 * m + 128])
                 sens = sensitivity(intensity, wide(target[:, start : start + 256]), doses)
-                cots.append(cotangent(e, sens))
-            for q, term in enumerate(back_columns(cots[0], cots[1], t_back, chunk)):
-                if chunk == 0:
-                    acc[q] = term
-                else:
-                    acc[q] += term
+                both.append(cotangent(e, sens))
+            cots[0, :, 256 * chunk : 256 * chunk + 256] = low(both[0] + both[1])
+            cots[1, :, 256 * chunk : 256 * chunk + 256] = low(both[0] - both[1])
         for q in range(2):
-            re, im = back_parts(acc[q])
+            re, im = back_parts(dot(cots[q], t_back[:, q * F : q * F + F]))
             for m in range(2):
                 lanes = slice(128 * m, 128 * m + 128)
                 tiles = regroup([re[:64, lanes], im[:64, lanes], re[64:, lanes], im[64:, lanes]])
@@ -426,10 +439,14 @@
             loads[5].wait()
         take(base + 3, r_db.at[step])
 
-        g = rows_spectrum(r_db[step], t_freq_b)
-        part = h_re[...] * g - h_im[...] * swap(g)
-        part = part + roll(part, 64)
-        s_d[step] = low(part)
+        early, late = wide(r_db[step, :32]), wide(r_db[step, 32:])
+        parts = []
+        for q, x in enumerate((early + late, early - late)):
+            rows = slice(q * EVEN, q * EVEN + EVEN)
+            g = rows_spectrum(x, t_freq_b, q)
+            part = h_re[rows, :] * g - h_im[rows, :] * swap(g)
+            parts.append(part + roll(part, 64))
+            s_d[step, rows, :] = low(parts[q])
         send(base + 4, s_d.at[step], r_d.at[step], sibling)
         if first:
             loads[6].wait()
@@ -442,10 +459,14 @@
                 return carry
 
             lax.fori_loop(1, KERNS, light_home, 0, unroll=True)
-        take(base + 4, r_d.at[step])
-        low_rows, high_rows = pixel_rows(part + wide(r_d[step]), t_rows_a)
-        s_da[step, :32] = side_by_side(low_rows)
-        s_da[step, 32:] = side_by_side(high_rows)
+        halves = []
+        for q in range(2):
+            rows = slice(q * EVEN, q * EVEN + EVEN)
+            if q == 0:
+                take(base + 4, r_d.at[step])
+            halves.append(pixel_rows(parts[q] + wide(r_d[step, rows, :]), t_rows_a, q))
+        s_da[step, :32] = side_by_side(halves[0] + halves[1])
+        s_da[step, 32:] = side_by_side(halves[0] - halves[1])
 
         def adjoint_out(x, y, da, db):
             to_z1, to_z0 = flip(z1, da), flip(z0, db)
@@ -457,37 +478,43 @@
         take(base + 5, r_da.at[step])
 
         own = grad_part(r_da[step], t_mix)
-        s_g[step] = own
-        send(base + 6, s_g.at[step], r_g.at[step], sibling)
-        take(base + 6, r_g.at[step])
-        other = r_g[step]
+        if last:
+            break
+        s_g[...] = own
+        send(base + 6, s_g, r_g, sibling)
+        take(base + 6, r_g)
+        other = r_g[...]
         lo = lo - step_rate * (own + other) * (1.0 - mask_lo * mask_lo)
         hi = hi - step_rate * (sign * (own - other)) * (1.0 - mask_hi * mask_hi)
+        mask_lo, mask_hi = jnp.tanh(lo), jnp.tanh(hi)
 
     for b in range(8):
-        s10[b] = lo[:, 128 * b : 128 * b + 128]
-        s10[b + 8] = hi[:, 128 * b : 128 * b + 128]
-    at_home = me_k // 8 == core
-    kern = 8 * core + me_k % 8
-    maybe_own(4, s10.at[kern], r10.at[kappa], (kern, me_s), at_home)
-
-    def params_home(t, carry):
-        kern = 8 * core + lax.rem(me_k + t, 8)
-        send(4, s10.at[kern], r10.at[kappa], (kern, me_s))
+        s11[b] = low(own[:, 128 * b : 128 * b + 128])
+
+    maybe_own(4, s11.at[me_k % 8], r11.at[core * 8 + kappa], (me_k, me_s), True)
+
+    def grad_home(t, carry):
+        kern = lax.rem(me_k + t, KERNS)
+        send(4, s11.at[kern % 8], r11.at[core * 8 + kappa], (kern, me_s))
         return carry
 
-    lax.fori_loop(1, 8, params_home, 0, unroll=True)
+    lax.fori_loop(1, KERNS, grad_home, 0, unroll=True)
     take(3, r9)
-    for k in range(KERNS):
-        light_out[k // 8, 16 * (k % 8) : 16 * (k % 8) + 16, :] = wide(r9[k])
-    take(4, r10)
-    params_out[...] = r10[...].reshape(128, 128)
+    light_out[...] = r9[...]
+    for n in range(STEPS - 1):
+        take(5 + 9 * STEPS + n, r10.at[n])
+    params_out[...] = r10[STEPS - 2]
+    take(4, r11)
+    grad_out[...] = r11[...]
 
     given(0, r0.at[pl.ds(0, KERNS - 1)])
     given(1, hr.at[pl.ds(0, 3)])
+    given(2, r_par.at[pl.ds(0, KERNS - 1)])
     given(3, s9.at[pl.ds(0, KERNS - 1)])
-    given(4, s10.at[pl.ds(0, 7)])
-    sent_maybe(4, s10.at[0], at_home)
+    given(4, r11.at[pl.ds(0, KERNS - 1)])
+    for n in range(STEPS - 1):
+        given(5 + 9 * STEPS + n, r10.at[n, pl.ds(0, 7)])
+        sent_maybe(5 + 9 * STEPS + n, r10.at[n, 0], at_home)
     for phase, is_own in sent:
         if is_own is True:
             given(phase, r_b.at[0, pl.ds(0, PEERS - 1)])
@@ -495,9 +522,22 @@
             given(phase, r_a.at[0, pl.ds(0, PEERS - 1)])
             sent_maybe(phase, r_a.at[0, 0], is_own)
     for step in range(STEPS):
-        given(5 + 7 * step + 1, s_sp.at[step])
-        given(5 + 7 * step + 4, s_d.at[step])
-        given(5 + 7 * step + 6, s_g.at[step])
+        given(5 + 9 * step + 1, s_sp.at[step])
+        given(5 + 9 * step + 4, s_d.at[step])
+        if step < STEPS - 1:
+            given(5 + 9 * step + 6, s_g)
+
+
+def finish(params_ref, grad_ref, light_ref, dose_ref, new_ref, printed_ref):
+    params = params_ref[...].reshape(128, 128)
+    mask = jnp.tanh(params)
+    even, odd = wide(grad_ref[:8]).reshape(128, 128), wide(grad_ref[8:]).reshape(128, 128)
+    sign = jnp.where(lax.axis_index("kern") < 8, 1.0, -1.0)
+    new_ref[...] = params - step_rate * (even + sign * odd) * (1.0 - mask * mask)
+    for c in range(2):
+        intensity = wide(light_ref[8 * c : 8 * c + 8]).reshape(128, 128)
+        for d in range(2):
+            printed_ref[c, d] = jax.nn.sigmoid(steepness * (dose_ref[d] * intensity - threshold))
 
 
 def body(mask_params, target_bits, kernels, weights, dose_factors):
@@ -513,14 +553,19 @@
         ((PEERS, 16, 128), (PEERS, 16, 128), bf16),
         ((F, 128), (F, 128), bf16),
         ((PEERS, 8, 128), (PEERS, 8, 128), bf16),
-        ((16, HALF), (16, HALF), f32),
     ):
         exchange += [pltpu.VMEM((STEPS,) + send_shape, kind), pltpu.VMEM((STEPS,) + shape, kind)]
-    params, intensity = pl.pallas_call(
+    exchange += [pltpu.VMEM((16, HALF), f32), pltpu.VMEM((16, HALF), f32)]
+    blocks = (
+        jax.ShapeDtypeStruct((8, 16, 128), f32),
+        jax.ShapeDtypeStruct((16, 16, 128), bf16),
+        jax.ShapeDtypeStruct((16, 16, 128), bf16),
+    )
+    home = pl.pallas_call(
         kernel,
-        out_shape=(jax.ShapeDtypeStruct((128, 128), f32), jax.ShapeDtypeStruct((2, 128, 128), f32)),
+        out_shape=blocks,
         in_specs=[hbm, hbm, hbm, smem, smem] + [hbm] * 6,
-        out_specs=(vmem, vmem),
+        out_specs=(vmem, vmem, vmem),
         scratch_shapes=[
             pltpu.VMEM((HALF, F), bf16),
             pltpu.VMEM((HALF, F), bf16),
@@ -535,29 +580,36 @@
             pltpu.VMEM((F, 128), f32),
             pltpu.VMEM((F, 128), f32),
             pltpu.VMEM((16, N), jnp.int32),
-            pltpu.VMEM((2, 256, F), f32),
+            pltpu.VMEM((2, 256, HALF), bf16),
+            pltpu.VMEM((128, 128), f32),
+            pltpu.VMEM((8, 16, 128), bf16),
+            pltpu.VMEM((16, 16, 128), bf16),
             pltpu.VMEM((16, 16, 128), f32),
             pltpu.VMEM((2, 32, F), bf16),
             pltpu.VMEM((4, 32, F), bf16),
             pltpu.VMEM((16, 16, 128), bf16),
             pltpu.VMEM((16, 16, 128), bf16),
             pltpu.VMEM((16, 16, 128), f32),
-            pltpu.VMEM((8, 16, 128), f32),
+            pltpu.VMEM((1, 8, 16, 128), f32),
+            pltpu.VMEM((8, 16, 128), bf16),
+            pltpu.VMEM((16, 16, 128), bf16),
         ]
         + exchange
         + [
             pltpu.SemaphoreType.DMA((11,)),
-            pltpu.SemaphoreType.DMA((19,)),
-            pltpu.SemaphoreType.DMA((19,)),
+            pltpu.SemaphoreType.DMA((24,)),
+            pltpu.SemaphoreType.DMA((24,)),
         ],
         compiler_params=pltpu.CompilerParams(
             collective_id=0, has_side_effects=True, vmem_limit_bytes=62 * 1024 * 1024
         ),
     )(mask_params, target_bits, kernels[0].transpose(0, 2, 1), weights, dose_factors, *consts)
-    printed = jax.nn.sigmoid(
-        steepness * (dose_factors[None, :, None, None] * intensity[:, None] - threshold)
-    )
-    return params, printed
+    return pl.pallas_call(
+        finish,
+        out_shape=(jax.ShapeDtypeStruct((128, 128), f32), jax.ShapeDtypeStruct((2, 2, 128, 128), f32)),
+        in_specs=[vmem, vmem, vmem, smem],
+        out_specs=(vmem, vmem),
+    )(*home, dose_factors)
 
 
 def solution(mesh):

time: 109 us -> 104 us (0.954)
  other arithmetic: 1.75 us -> 0 us
  local copies, waits for them, and re-layouts: 1.48 us -> 0 us
    div x1 -> x0, other arithmetic: 1.75 us -> none  [body(): jax.nn.sigmoid(steepness * (dose_factors[None, :, None, None] * intensity...]
    unnamed x3 -> x0, local copies, waits for them, and re-layouts: 1.48 us -> none
    pallas_call x1 -> x2, Pallas kernels: 104 us -> 103 us  [the longest x1 101 us: body(): pl.pallas_call(kernel, out_shape=blocks, in_specs=[hbm, hbm, hbm, smem, s...]
where the time goes in v5:
time: 104 us
  Pallas kernels  103 us (99%)
  between operations  1.28 us (1%)
    pallas_call x1, Pallas kernels, body(): pl.pallas_call(kernel, out_shape=blocks, in_specs=[hbm, hbm, hbm, smem, s...  101 us

profile of v5, /device:TPU:1, one launch (start us, length us, event | category | flops | bytes accessed | tf_op | source)
XLA Modules:
  0.0 104.2 jit_solution(16783955200267191089)
XLA Ops:
  1.3 101.2 %shard_map.122 = (f32[8,16,128]{2,1,0:T(8,128)}, bf16[16,16,128]{2,1,0:T(8,128)(2,1)}, bf16[16,16,128]{2,1,0:T(8,128)(2,1)}) custom-call(f32[128,128]{1,0:T(8,128)} %mask_hbm.1, s32[128,2048]{1,0:T(8,128)} %target_hbm.1, f32[2,32,512]{2,1,0:T(8,128)} %bitcast.3, f32[1]{0:T(128)S(6)} %copy.13.weight_ref, f32[2]{0:T(128)} %dose_ref.3, ...), custom_call_target="tpu_custom_call" | custom-call | tf_op jit(solution)/shard_map/pallas_call | solution.py:564
  102.5 1.7 %shard_map.123 = (f32[128,128]{1,0:T(8,128)}, f32[2,2,128,128]{3,2,1,0:T(8,128)}) custom-call(f32[8,16,128]{2,1,0:T(8,128)} %get-tuple-element.5.params_ref, bf16[16,16,128]{2,1,0:T(8,128)(2,1)} %get-tuple-element.6.grad_ref, bf16[16,16,128]{2,1,0:T(8,128)(2,1)} %get-tuple-element.7.light_ref, f32[2]{0:T(128)} %dose_ref.3), custom_call_target="tpu_custom_call" | custom-call | tf_op jit(solution)/shard_map/pallas_call | solution.py:607

commit v6 on v5

--- a/solution.py
+++ b/solution.py
@@ -188,12 +188,15 @@
     barrier = pltpu.get_barrier_semaphore()
 
     def greet(t, carry):
-        slab = lax.rem(me_s + t, SLABS)
         kern = lax.rem(me_k + t, KERNS)
-        pl.semaphore_signal(barrier, inc=1, device_id=(me_k, slab), device_id_type=MESH)
         pl.semaphore_signal(barrier, inc=1, device_id=(kern, me_s), device_id_type=MESH)
         return carry
 
+    for dy in (2, 1, 3, 0):
+        for dz in (2, 1, 3, 0):
+            if dy or dz:
+                slab = 4 * lax.rem(y_at + dy, 4) + lax.rem(me_s + dz, 4)
+                pl.semaphore_signal(barrier, inc=1, device_id=(me_k, slab), device_id_type=MESH)
     pl.semaphore_signal(
         barrier, inc=1, device_id=device(x_at, y_at, 1 - z2, z1, 1 - z0, core), device_id_type=MESH
     )
@@ -312,7 +315,6 @@
         else:
             maybe_own(1, hs.at[to_par], hr.at[2 * z0 + z2], where, True)
 
-    lax.fori_loop(1, KERNS, out_params, 0, unroll=True)
     r_par[me_k] = home[pl.ds(pl.multiple_of(16 * kappa, 16), 16), :]
     take(0, r0.at[pl.ds(0, KERNS - 1)])
     mask_lo = wide(jnp.concatenate([r0[b] for b in range(8)], 1))
@@ -338,6 +340,8 @@
             return s_a.at[step, 2 * y + to_z1], device(x, y, flip(z2, da), to_z1, core, z2)
 
         direct(base, columns_out, r_a.at[step, place], owner_is_reader)
+        if first:
+            lax.fori_loop(1, KERNS, out_params, 0, unroll=True)
         if last:
             for b in range(8):
                 s10[b] = lo[:, 128 * b : 128 * b + 128]

time: 104 us -> 104 us (level)
  no operation moved by 1% of the time
where the time goes in v6:
time: 104 us
  Pallas kernels  102 us (98%)
  between operations  1.28 us (1%)
    pallas_call x1, Pallas kernels, body(): pl.pallas_call(kernel, out_shape=blocks, in_specs=[hbm, hbm, hbm, smem, s...  101 us

profile of v6, /device:TPU:1, one launch (start us, length us, event | category | flops | bytes accessed | tf_op | source)
XLA Modules:
  0.0 103.7 jit_solution(2538171368103431355)
XLA Ops:
  1.3 100.7 %shard_map.122 = (f32[8,16,128]{2,1,0:T(8,128)}, bf16[16,16,128]{2,1,0:T(8,128)(2,1)}, bf16[16,16,128]{2,1,0:T(8,128)(2,1)}) custom-call(f32[128,128]{1,0:T(8,128)} %mask_hbm.1, s32[128,2048]{1,0:T(8,128)} %target_hbm.1, f32[2,32,512]{2,1,0:T(8,128)} %bitcast.3, f32[1]{0:T(128)S(6)} %copy.13.weight_ref, f32[2]{0:T(128)} %dose_ref.3, ...), custom_call_target="tpu_custom_call" | custom-call | tf_op jit(solution)/shard_map/pallas_call | solution.py:568
  102.0 1.7 %shard_map.123 = (f32[128,128]{1,0:T(8,128)}, f32[2,2,128,128]{3,2,1,0:T(8,128)}) custom-call(f32[8,16,128]{2,1,0:T(8,128)} %get-tuple-element.5.params_ref, bf16[16,16,128]{2,1,0:T(8,128)(2,1)} %get-tuple-element.6.grad_ref, bf16[16,16,128]{2,1,0:T(8,128)(2,1)} %get-tuple-element.7.light_ref, f32[2]{0:T(128)} %dose_ref.3), custom_call_target="tpu_custom_call" | custom-call | tf_op jit(solution)/shard_map/pallas_call | solution.py:611

commit v7 on v6

--- a/solution.py
+++ b/solution.py
@@ -340,8 +340,6 @@
             return s_a.at[step, 2 * y + to_z1], device(x, y, flip(z2, da), to_z1, core, z2)
 
         direct(base, columns_out, r_a.at[step, place], owner_is_reader)
-        if first:
-            lax.fori_loop(1, KERNS, out_params, 0, unroll=True)
         if last:
             for b in range(8):
                 s10[b] = lo[:, 128 * b : 128 * b + 128]
@@ -355,20 +353,6 @@
                 return carry
 
             lax.fori_loop(1, 8, params_home, 0, unroll=True)
-        if first:
-            loads[1].wait()
-            take(2, r_par.at[pl.ds(0, KERNS - 1)])
-            lo = jnp.concatenate([r_par[b] for b in range(8)], 1)
-            hi = jnp.concatenate([r_par[b] for b in range(8, 16)], 1)
-            mask_lo, mask_hi = jnp.tanh(lo), jnp.tanh(hi)
-        take(base, r_a.at[step])
-        early, late = wide(r_a[step, :32].reshape(256, 128)), wide(r_a[step, 32:].reshape(256, 128))
-        parts = []
-        for q, x in enumerate((early + late, early - late)):
-            rows = slice(q * EVEN, q * EVEN + EVEN)
-            parts.append(columns_spectrum(x, t_freq_a, q))
-            s_sp[step, rows, :] = low(parts[q])
-        send(base + 1, s_sp.at[step], r_sp.at[step], sibling)
         if first:
             take(1, hr)
             flat = jnp.concatenate(
@@ -382,6 +366,15 @@
                 h_re[rows, :] = jnp.where(is_real(h), h, swapped)
                 h_im[rows, :] = jnp.where(is_real(h), -swapped, h)
             loads[2].wait()
+            loads[1].wait()
+        take(base, r_a.at[step])
+        early, late = wide(r_a[step, :32].reshape(256, 128)), wide(r_a[step, 32:].reshape(256, 128))
+        parts = []
+        for q, x in enumerate((early + late, early - late)):
+            rows = slice(q * EVEN, q * EVEN + EVEN)
+            parts.append(columns_spectrum(x, t_freq_a, q))
+            s_sp[step, rows, :] = low(parts[q])
+        send(base + 1, s_sp.at[step], r_sp.at[step], sibling)
 
         halves = []
         for q in range(2):
@@ -440,6 +433,7 @@
 
         direct(base + 3, back_out, r_db.at[step, place], True)
         if first:
+            lax.fori_loop(1, KERNS, out_params, 0, unroll=True)
             loads[5].wait()
         take(base + 3, r_db.at[step])
 
@@ -479,6 +473,10 @@
         direct(base + 5, adjoint_out, r_da.at[step, block * 8 + z2 * 4 + x_at], owner_is_reader)
         if first:
             loads[7].wait()
+            take(2, r_par.at[pl.ds(0, KERNS - 1)])
+            lo = jnp.concatenate([r_par[b] for b in range(8)], 1)
+            hi = jnp.concatenate([r_par[b] for b in range(8, 16)], 1)
+            mask_lo, mask_hi = jnp.tanh(lo), jnp.tanh(hi)
         take(base + 5, r_da.at[step])
 
         own = grad_part(r_da[step], t_mix)

time: 104 us -> 103 us (level)
  no operation moved by 1% of the time
where the time goes in v7:
time: 103 us
  Pallas kernels  102 us (99%)
  between operations  1.28 us (1%)
    pallas_call x1, Pallas kernels, body(): pl.pallas_call(kernel, out_shape=blocks, in_specs=[hbm, hbm, hbm, smem, s...  100 us

profile of v7, /device:TPU:1, one launch (start us, length us, event | category | flops | bytes accessed | tf_op | source)
XLA Modules:
  0.0 103.3 jit_solution(17375843814788124377)
XLA Ops:
  1.3 100.3 %shard_map.122 = (f32[8,16,128]{2,1,0:T(8,128)}, bf16[16,16,128]{2,1,0:T(8,128)(2,1)}, bf16[16,16,128]{2,1,0:T(8,128)(2,1)}) custom-call(f32[128,128]{1,0:T(8,128)} %mask_hbm.1, s32[128,2048]{1,0:T(8,128)} %target_hbm.1, f32[2,32,512]{2,1,0:T(8,128)} %bitcast.3, f32[1]{0:T(128)S(6)} %copy.13.weight_ref, f32[2]{0:T(128)} %dose_ref.3, ...), custom_call_target="tpu_custom_call" | custom-call | tf_op jit(solution)/shard_map/pallas_call | solution.py:566
  101.6 1.7 %shard_map.123 = (f32[128,128]{1,0:T(8,128)}, f32[2,2,128,128]{3,2,1,0:T(8,128)}) custom-call(f32[8,16,128]{2,1,0:T(8,128)} %get-tuple-element.5.params_ref, bf16[16,16,128]{2,1,0:T(8,128)(2,1)} %get-tuple-element.6.grad_ref, bf16[16,16,128]{2,1,0:T(8,128)(2,1)} %get-tuple-element.7.light_ref, f32[2]{0:T(128)} %dose_ref.3), custom_call_target="tpu_custom_call" | custom-call | tf_op jit(solution)/shard_map/pallas_call | solution.py:609
